TPU v7x, 32 devices: a whole 2x2x4 slice. The times are simulated.
32 devices in a mesh: seq: 4 (over z), dp: 8 (over y, x, core).
Axes of the slice: x: 2, y: 2, z: 4, core: 2. Of those that a mesh axis runs over, the one named last changes fastest.
Arguments:
- block_input: float32 [192, 1024, 768], P('dp', 'seq'), may hold values from -800 to 800
- first_gain: float32 [768], replicated, may hold values from 0.1 to 1.9
- first_shift: float32 [768], replicated, may hold values from -3 to 3
- dilated_weight: float32 [3, 768, 384], replicated, may hold values from -0.125 to 0.125
- second_gain: float32 [384], replicated, may hold values from 0.1 to 1.9
- second_shift: float32 [384], replicated, may hold values from -3 to 3
- point_weight: float32 [384, 768], replicated, may hold values from -0.3125 to 0.3125
- cotangent: float32 [192, 1024, 768], P('dp', 'seq'), may hold values from -6 to 6
Outputs:
- block_output: float32 [192, 1024, 768], P('dp', 'seq')
- input_grad: float32 [192, 1024, 768], P('dp', 'seq')
- first_gain_grad: float32 [768], replicated
- first_shift_grad: float32 [768], replicated
- dilated_grad: float32 [3, 768, 384], replicated
- second_gain_grad: float32 [384], replicated
- second_shift_grad: float32 [384], replicated
- point_grad: float32 [384, 768], replicated
All inputs are finite; a program needn't handle non-finite values.
Results may differ from a plain program's by a relative error of at most 0.0003.
Values sent between devices are 32-bit elements; how exact they have to be, the bound alone decides.
No kernel may reach another device: no remote copies, remote signals or barrier semaphores. Data moves between devices by JAX's collectives and lax.ppermute only.
A program may use at most 256 MiB of HBM per device.

v0:
```python
import jax
import jax.numpy as jnp
from jax import lax
from jax.sharding import PartitionSpec as P

DILATION_STEP = 57


EPS = 1e-05
INV_ROOT_TWO = 0.7071067811865476
INV_ROOT_TWO_PI = 0.3989422804014327


def padded(cells, sides, width):
    for axis, dim in sides:
        count = lax.axis_size(axis)
        ends = count - 1
        head = lax.slice_in_dim(cells, 0, width, axis=dim)
        tail = lax.slice_in_dim(cells, cells.shape[dim] - width, cells.shape[dim], axis=dim)
        cells = jnp.concatenate(
            [
                lax.ppermute(tail, axis, [(i, (i + 1) % count) for i in range(ends)]),
                cells,
                lax.ppermute(head, axis, [((i + 1) % count, i) for i in range(ends)]),
            ],
            axis=dim,
        )
    return cells


def from_behind(array, axis, by):
    count = lax.axis_size(axis)
    pairs = [(i, i + by) for i in range(count) if 0 <= i + by < count]
    return lax.ppermute(array, axis, pairs)


def gelu_value(feature_values):
    return 0.5 * feature_values * (1.0 + lax.erf(feature_values * INV_ROOT_TWO))


def gelu_slope(feature_values):
    return (
        0.5 * (1.0 + lax.erf(feature_values * INV_ROOT_TWO))
        + feature_values * jnp.exp(-0.5 * feature_values * feature_values) * INV_ROOT_TWO_PI
    )


def moments(feature_values, total_bins):
    center = lax.psum(jnp.sum(feature_values, axis=(0, 1)), ("seq", "dp")) / total_bins
    offset = feature_values - center
    spread = lax.psum(jnp.sum(offset * offset, axis=(0, 1)), ("seq", "dp")) / total_bins
    inverse = lax.rsqrt(spread + EPS)
    return ((feature_values - center) * inverse, inverse)


def norm_back(upstream, normed, gain, inverse, total_bins):
    shift_grad, gain_grad = lax.psum(
        (jnp.sum(upstream, axis=(0, 1)), jnp.sum(upstream * normed, axis=(0, 1))), ("seq", "dp")
    )
    downward = (
        gain * inverse * (upstream - shift_grad / total_bins - normed * (gain_grad / total_bins))
    )
    return (downward, gain_grad, shift_grad)


def tap_product(left, right, form):
    return jnp.einsum(
        form, left, right, precision=lax.Precision.HIGHEST, preferred_element_type=jnp.float32
    )


def taps_from_padded(padded_input, kernel_weight, bins_per_shard):
    middle_features = tap_product(
        padded_input[:, 0:bins_per_shard], kernel_weight[0], "oxi,ik->oxk"
    )
    middle_features = middle_features + tap_product(
        padded_input[:, DILATION_STEP : DILATION_STEP + bins_per_shard],
        kernel_weight[1],
        "oxi,ik->oxk",
    )
    return middle_features + tap_product(
        padded_input[:, 2 * DILATION_STEP : 2 * DILATION_STEP + bins_per_shard],
        kernel_weight[2],
        "oxi,ik->oxk",
    )


def on_device(
    block_input,
    first_gain,
    first_shift,
    dilated_weight,
    second_gain,
    second_shift,
    point_weight,
    cotangent,
):
    shifted_windows, bins_per_shard, channel_count = block_input.shape
    total_bins = float(
        shifted_windows * bins_per_shard * lax.axis_size("seq") * lax.axis_size("dp")
    )
    normed_first, inverse_first = moments(block_input, total_bins)
    pre_first = first_gain * normed_first + first_shift
    first_activation = gelu_value(pre_first)
    padded_input = padded(first_activation, (("seq", 1),), DILATION_STEP)
    middle_features = taps_from_padded(padded_input, dilated_weight, bins_per_shard)
    normed_second, inverse_second = moments(middle_features, total_bins)
    pre_second = second_gain * normed_second + second_shift
    act_second = gelu_value(pre_second)
    block_output = block_input + tap_product(act_second, point_weight, "wbm,mc->wbc")
    point_grad = tap_product(act_second, cotangent, "wbm,wbc->mc")
    up_second = tap_product(cotangent, point_weight, "wbc,mc->wbm") * gelu_slope(pre_second)
    middle_features_gradient, second_gain_grad, second_shift_grad = norm_back(
        up_second, normed_second, second_gain, inverse_second, total_bins
    )
    dilated_grad = jnp.stack(
        [
            tap_product(
                padded_input[
                    :,
                    kernel_tap_index * DILATION_STEP : kernel_tap_index * DILATION_STEP
                    + bins_per_shard,
                ],
                middle_features_gradient,
                "ohr,ohl->rl",
            )
            for kernel_tap_index in range(3)
        ]
    )
    variance_gradient = jnp.zeros(
        (shifted_windows, bins_per_shard + 2 * DILATION_STEP, channel_count), jnp.float32
    )
    for kernel_tap_index in range(3):
        variance_gradient = variance_gradient.at[
            :, kernel_tap_index * DILATION_STEP : kernel_tap_index * DILATION_STEP + bins_per_shard
        ].add(
            tap_product(middle_features_gradient, dilated_weight[kernel_tap_index], "wbm,cm->wbc")
        )
    next_neighbor_gradient = from_behind(variance_gradient[:, 0:DILATION_STEP], "seq", -1)
    previous_neighbor_gradient = from_behind(
        variance_gradient[:, bins_per_shard + DILATION_STEP :], "seq", 1
    )
    activation_gradient = variance_gradient[:, DILATION_STEP : DILATION_STEP + bins_per_shard]
    activation_gradient = (
        activation_gradient.at[:, bins_per_shard - DILATION_STEP :]
        .add(next_neighbor_gradient)
        .at[:, 0:DILATION_STEP]
        .add(previous_neighbor_gradient)
    )
    up_first = activation_gradient * gelu_slope(pre_first)
    input_part, first_gain_grad, first_shift_grad = norm_back(
        up_first, normed_first, first_gain, inverse_first, total_bins
    )
    input_grad = cotangent + input_part
    dilated_grad, point_grad = lax.psum((dilated_grad, point_grad), ("seq", "dp"))
    return (
        block_output,
        input_grad,
        first_gain_grad,
        first_shift_grad,
        dilated_grad,
        second_gain_grad,
        second_shift_grad,
        point_grad,
    )


def solution(mesh):
    return jax.shard_map(
        on_device,
        mesh=mesh,
        in_specs=(P("dp", "seq", None), P(), P(), P(), P(), P(), P(), P("dp", "seq", None)),
        out_specs=(P("dp", "seq", None), P("dp", "seq", None), P(), P(), P(), P(), P(), P()),
        check_vma=False,
    )
```

profile of v0, /device:TPU:0, one launch (start us, length us, event | category | flops | bytes accessed | tf_op | source)
XLA Modules:
  0.0 1086.0 jit_solution(1789646230539013983)
XLA Ops:
  14.7 42.0 %psum.70 = f32[768]{0:T(1024)S(1)} all-reduce(f32[768]{0:T(1024)S(1)} %reduce_sum.72), channel_id=1, replica_groups=mesh['seq'=4,'dp'=8] {'seq','dp'}, use_global_device_ids=true, to_apply=%region_1.0 | all-reduce | flops 768 | bytes 6144 | tf_op jit(solution)/shard_map/psum | solution.py:49
  65.0 40.2 %psum.71 = f32[768]{0:T(1024)S(1)} all-reduce(f32[768]{0:T(1024)S(1)} %multiply_reduce_fusion.1), channel_id=1, replica_groups=mesh['seq'=4,'dp'=8] {'seq','dp'}, use_global_device_ids=true, to_apply=%region_3.0 | all-reduce | flops 768 | bytes 6144 | tf_op jit(solution)/shard_map/psum | solution.py:51
  146.8 32.0 %fusion.23 = f32[24,256,384]{2,1,0:T(8,128)} fusion(f32[24,256,768]{2,1,0:T(8,128)S(1)} %bitcast.51, f32[3,768,384]{2,1,0:T(8,128)S(1)} %copy-done.4), kind=kOutput, calls=%fused_computation.48 | convolution fusion | flops 21743271936 | bytes 29491200 | tf_op jit(solution)/shard_map/oxi,ik->oxk/dot_general | solution.py:67
  178.9 49.5 %collective-permute-done = f32[24,57,768]{2,0,1:T(8,128)} collective-permute-done((f32[24,57,768]{2,0,1:T(8,128)}, f32[24,57,768]{2,0,1:T(8,128)}, u32[]{:S(2)}, u32[]{:S(2)}) %collective-permute-start) | collective-permute-done | bytes 4202528 | tf_op jit(solution)/shard_map/ppermute | solution.py:22
  232.0 32.5 %fusion.5 = f32[24,256,384]{2,1,0:T(8,128)} fusion(f32[24,256,768]{2,1,0:T(8,128)S(1)} %bitcast.51, f32[24,57,768]{2,1,0:T(8,128)S(1)} %copy.21, f32[3,768,384]{2,1,0:T(8,128)S(1)} %copy-done.4), kind=kOutput, calls=%fused_computation.18 | convolution fusion | flops 21747990528 | bytes 34209792 | tf_op jit(solution)/shard_map/oxi,ik->oxk/dot_general | solution.py:67
  268.1 40.5 %fusion.47 = (f32[384]{0:T(512)S(1)}, f32[24,256,384]{2,1,0:T(8,128)}) fusion(f32[3,768,384]{2,1,0:T(8,128)} %param.21, f32[24,57,768]{2,1,0:T(8,128)S(1)} %copy.23, f32[24,256,768]{2,1,0:T(8,128)S(1)} %bitcast.51, f32[24,256,384]{2,1,0:T(8,128)} %fusion.5, f32[24,256,384]{2,1,0:T(8,128)} %fusion.23), kind=kOutput, calls=%fused_computation.79 | convolution fusion | flops 21755068416 | bytes 52569600 | tf_op jit(solution)/shard_map/oxi,ik->oxk/dot_general | solution.py:67
  308.6 41.0 %psum.72 = f32[384]{0:T(512)S(1)} all-reduce(f32[384]{0:T(512)S(1)} %get-tuple-element.87), channel_id=1, replica_groups=mesh['seq'=4,'dp'=8] {'seq','dp'}, use_global_device_ids=true, to_apply=%region_5.0 | all-reduce | flops 384 | bytes 3072 | tf_op jit(solution)/shard_map/psum | solution.py:49
  354.4 41.2 %psum.73 = f32[384]{0:T(512)S(1)} all-reduce(f32[384]{0:T(512)S(1)} %multiply_reduce_fusion.3), channel_id=1, replica_groups=mesh['seq'=4,'dp'=8] {'seq','dp'}, use_global_device_ids=true, to_apply=%region_7.0 | all-reduce | flops 384 | bytes 3072 | tf_op jit(solution)/shard_map/psum | solution.py:51
  395.7 39.2 %fusion.43 = (f32[384]{0:T(512)S(1)}, f32[384]{0:T(512)S(1)}, f32[24,256,384]{2,1,0:T(8,128)}) fusion(f32[384]{0:T(512)S(1)} %get-tuple-element.86, f32[24,256,384]{2,1,0:T(8,128)} %get-tuple-element.88, f32[384]{0:T(512)S(1)} %broadcast_multiply_fusion.5, f32[384]{0:T(512)S(1)} %copy-done.17, f32[384]{0:T(512)S(1)} %copy-done.12, ...), kind=kOutput, calls=%fused_computation.76 | convolution fusion | flops 21781020672 | bytes 38937600 | tf_op jit(solution)/shard_map/wbc,mc->wbm/dot_general | solution.py:67
  434.9 39.1 %all-reduce.2 = (f32[384]{0:T(512)S(1)}, f32[384]{0:T(512)S(1)}) all-reduce(f32[384]{0:T(512)S(1)} %get-tuple-element.71, f32[384]{0:T(512)S(1)} %get-tuple-element.70), channel_id=1, replica_groups=mesh['seq'=4,'dp'=8] {'seq','dp'}, use_global_device_ids=true, to_apply=%region_11.0 | all-reduce | flops 768 | bytes 6144 | tf_op jit(solution)/shard_map/psum | solution.py:57
  486.8 36.6 %fusion.25 = f32[24,256,768]{2,1,0:T(8,128)S(1)} fusion(f32[24,256,384]{2,1,0:T(8,128)} %subtract_multiply_fusion.1, f32[3,768,384]{2,1,0:T(8,128)} %param.21), kind=kOutput, calls=%fused_computation.50 | convolution fusion | flops 21743271936 | bytes 29491200 | tf_op jit(solution)/shard_map/wbm,cm->wbc/dot_general | solution.py:67
  523.4 35.7 %slice_add_fusion.1 = f32[24,256,768]{2,1,0:T(8,128)} fusion(f32[24,256,384]{2,1,0:T(8,128)S(1)} %copy-done.1, f32[24,256,768]{2,1,0:T(8,128)S(1)} %fusion.25, f32[3,768,384]{2,1,0:T(8,128)} %param.21), kind=kOutput, calls=%fused_computation.11 | convolution fusion | flops 21747990528 | bytes 48365568 | tf_op jit(solution)/shard_map/wbm,cm->wbc/dot_general | solution.py:67
  568.6 46.2 %scatter-add.19 = f32[24,370,768]{2,1,0:T(8,128)} dynamic-update-slice(f32[24,370,768]{2,1,0:T(8,128)} %scatter-add.16, f32[24,256,768]{2,1,0:T(8,128)} %slice_add_fusion.1, s32[]{:T(128)} %constant.161.clone.1, s32[]{:T(128)} %constant.162.clone.1, s32[]{:T(128)} %constant.161.clone.1) | dynamic-update-slice | bytes 37748740 | tf_op jit(solution)/shard_map/scatter-add | solution.py:136
  614.8 36.5 %slice_add_fusion = f32[24,256,768]{2,1,0:T(8,128)} fusion(f32[24,370,768]{2,1,0:T(8,128)} %scatter-add.19, f32[24,256,384]{2,1,0:T(8,128)} %subtract_multiply_fusion.1, f32[3,768,384]{2,1,0:T(8,128)} %param.21), kind=kOutput, calls=%fused_computation.6 | convolution fusion | flops 21747990528 | bytes 48365568 | tf_op jit(solution)/shard_map/wbm,cm->wbc/dot_general | solution.py:67
  651.3 46.1 %scatter-add.20 = f32[24,370,768]{2,1,0:T(8,128)} dynamic-update-slice(f32[24,370,768]{2,1,0:T(8,128)} %scatter-add.19, f32[24,256,768]{2,1,0:T(8,128)} %slice_add_fusion, s32[]{:T(128)} %constant.161.clone.1, s32[]{:T(128)} %constant.163.clone.1, s32[]{:T(128)} %constant.161.clone.1) | dynamic-update-slice | bytes 37748740 | tf_op jit(solution)/shard_map/scatter-add | solution.py:136
  706.2 35.1 %fusion.14 = f32[1,768,384]{2,1,0:T(8,128)S(1)} fusion(f32[24,256,384]{2,1,0:T(8,128)} %subtract_multiply_fusion.1, f32[24,57,768]{2,1,0:T(8,128)} %copy-done.3, f32[24,256,768]{2,1,0:T(8,128)} %multiply_multiply_fusion.1), kind=kOutput, calls=%fused_computation.41 | convolution fusion | flops 21747990528 | bytes 33693696 | tf_op jit(solution)/shard_map/ohr,ohl->rl/dot_general | solution.py:67
  741.4 32.5 %convolution_bitcast_fusion.1 = f32[1,768,384]{2,1,0:T(8,128)S(1)} fusion(f32[24,256,768]{2,1,0:T(8,128)S(1)} %bitcast.53, f32[24,256,384]{2,1,0:T(8,128)} %subtract_multiply_fusion.1), kind=kOutput, calls=%fused_computation.40 | convolution fusion | flops 21743271936 | bytes 29491200 | tf_op jit(solution)/shard_map/ohr,ohl->rl/dot_general | solution.py:67
  773.9 25.0 %collective-permute-done.2 = f32[24,57,768]{2,0,1:T(8,128)} collective-permute-done((f32[24,57,768]{2,0,1:T(8,128)}, f32[24,57,768]{2,0,1:T(8,128)}, u32[]{:S(2)}, u32[]{:S(2)}) %collective-permute-start.2) | collective-permute-done | bytes 4202528 | tf_op jit(solution)/shard_map/ppermute | solution.py:34
  822.3 34.1 %fusion.15 = f32[1,768,384]{2,1,0:T(8,128)} fusion(f32[24,256,384]{2,1,0:T(8,128)} %subtract_multiply_fusion.1, f32[24,256,768]{2,1,0:T(8,128)} %multiply_multiply_fusion.1, f32[24,57,768]{2,1,0:T(8,128)S(1)} %bitcast.57), kind=kOutput, calls=%fused_computation.42 | convolution fusion | flops 21747990528 | bytes 33693696 | tf_op jit(solution)/shard_map/ohr,ohl->rl/dot_general | solution.py:67
  874.3 27.8 %convolution_bitcast_fusion = f32[384,768]{1,0:T(8,128)} fusion(f32[24,256,768]{2,1,0:T(8,128)S(1)} %bitcast.59, f32[24,256,384]{2,1,0:T(8,128)S(1)} %bitcast.55, f32[384]{0:T(512)S(1)} %copy-done.18, f32[384]{0:T(512)S(1)} %get-tuple-element.86, f32[384]{0:T(512)S(1)} %broadcast_multiply_fusion.5, f32[384]{0:T(512)S(1)} %copy-done.13), kind=kOutput, calls=%fused_computation.39 | convolution fusion | flops 21762146304 | bytes 29497344 | tf_op jit(solution)/shard_map/wbm,wbc->mc/dot_general | solution.py:67
  902.1 38.6 %convolution_add_fusion = f32[24,256,768]{2,1,0:T(8,128)} fusion(f32[24,256,768]{2,1,0:T(8,128)} %param.18, f32[24,256,384]{2,1,0:T(8,128)} %get-tuple-element.88, f32[384]{0:T(512)S(1)} %copy-done.18, f32[384]{0:T(512)S(1)} %get-tuple-element.86, f32[384]{0:T(512)S(1)} %broadcast_multiply_fusion.5, f32[384]{0:T(512)S(1)} %copy-done.13, ...), kind=kOutput, calls=%fused_computation.35 | convolution fusion | flops 21766864896 | bytes 48371712 | tf_op jit(solution)/shard_map/wbm,mc->wbc/dot_general | solution.py:67
  983.2 25.3 %fusion.42 = (f32[768]{0:T(1024)S(1)}, f32[768]{0:T(1024)S(1)}, f32[24,256,768]{2,1,0:T(8,128)}) fusion(f32[768]{0:T(1024)S(1)} %copy-done.9, f32[24,256,768]{2,1,0:T(8,128)} %param.18, f32[768]{0:T(1024)S(1)} %copy-done.7, f32[24,256,768]{2,1,0:T(8,128)} %scatter-add.24, f32[768]{0:T(1024)S(1)} %copy-done.15, f32[768]{0:T(1024)S(1)} %copy-done.11), kind=kLoop, calls=%fused_computation.75 | loop fusion | flops 75495936 | bytes 56641536 | tf_op jit(solution)/shard_map/reduce_sum | solution.py:58
  1008.5 38.5 %all-reduce.1 = (f32[768]{0:T(1024)S(1)}, f32[768]{0:T(1024)S(1)}) all-reduce(f32[768]{0:T(1024)S(1)} %get-tuple-element.69, f32[768]{0:T(1024)S(1)} %get-tuple-element.68), channel_id=1, replica_groups=mesh['seq'=4,'dp'=8] {'seq','dp'}, use_global_device_ids=true, to_apply=%region_15.0 | all-reduce | flops 1536 | bytes 12288 | tf_op jit(solution)/shard_map/psum | solution.py:57
  1047.0 25.5 %multiply_add_fusion = f32[24,256,768]{2,1,0:T(8,128)} fusion(f32[24,256,768]{2,1,0:T(8,128)} %param.25, f32[24,256,768]{2,1,0:T(8,128)} %get-tuple-element.78, f32[24,256,768]{2,1,0:T(8,128)} %param.18, f32[768]{0:T(1024)S(1)} %broadcast_multiply_fusion, f32[768]{0:T(1024)S(1)} %broadcast_multiply_fusion.1, f32[768]{0:T(1024)S(1)} %copy-done.16, ...), kind=kLoop, calls=%fused_computation.9 | loop fusion | flops 33030144 | bytes 75512832 | tf_op jit(solution)/shard_map/add | solution.py:154
  (129 shorter events, 190.6 us)
Async XLA Ops:
  7.2 388.5 %copy-start = (f32[384,768]{1,0:T(8,128)S(1)}, f32[384,768]{1,0:T(8,128)}, u32[]{:S(2)}) copy-start(f32[384,768]{1,0:T(8,128)} %param.24) | copy-start | bytes 3538948
  7.2 1065.4 %all-reduce.6.cloned.1.call-start = ((), (), s32[]{:S(2)}) async-start(), calls=%async_computation | async-start | bytes 9437184 | tf_op jit(solution)/shard_map/psum | solution.py:155
  56.7 49.1 %copy-start.6 = (f32[768]{0:T(1024)}, f32[768]{0:T(1024)S(1)}, u32[]{:S(2)}) copy-start(f32[768]{0:T(1024)S(1)} %broadcast_multiply_fusion.2) | copy-start | bytes 9220
  56.7 48.5 %copy-start.10 = (f32[768]{0:T(1024)S(1)}, f32[768]{0:T(1024)}, u32[]{:S(2)}) copy-start(f32[768]{0:T(1024)} %param.19) | copy-start | bytes 9220
  56.7 49.7 %copy-start.14 = (f32[768]{0:T(1024)S(1)}, f32[768]{0:T(1024)}, u32[]{:S(2)}) copy-start(f32[768]{0:T(1024)} %param.20) | copy-start | bytes 9220
  136.5 91.9 %collective-permute-start = (f32[24,57,768]{2,0,1:T(8,128)}, f32[24,57,768]{2,0,1:T(8,128)}, u32[]{:S(2)}, u32[]{:S(2)}) collective-permute-start(f32[24,57,768]{2,0,1:T(8,128)} %copy.20), channel_id=1, source_target_pairs={{0,8},{8,16},{16,24},{1,9},{9,17},{17,25},{2,10},{10,18},{18,26},{... | collective-permute-start | bytes 12607496 | tf_op jit(solution)/shard_map/ppermute | solution.py:22
  145.3 119.2 %collective-permute-start.1 = (f32[24,57,768]{2,0,1:T(8,128)}, f32[24,57,768]{2,0,1:T(8,128)}, u32[]{:S(2)}, u32[]{:S(2)}) collective-permute-start(f32[24,57,768]{2,0,1:T(8,128)} %copy.22), channel_id=1, source_target_pairs={{8,0},{16,8},{24,16},{9,1},{17,9},{25,17},{10,2},{18,10},{26,18},{... | collective-permute-start | bytes 12607496 | tf_op jit(solution)/shard_map/ppermute | solution.py:24
  268.1 40.5 %copy-start.3 = (f32[24,57,768]{2,1,0:T(8,128)}, f32[24,57,768]{2,1,0:T(8,128)S(1)}, u32[]{:S(2)}) copy-start(f32[24,57,768]{2,1,0:T(8,128)S(1)} %copy.23) | copy-start | bytes 12607492
  308.6 87.0 %copy-start.12 = (f32[384]{0:T(512)S(1)}, f32[384]{0:T(512)}, u32[]{:S(2)}) copy-start(f32[384]{0:T(512)} %param.22) | copy-start | bytes 4612
  308.6 87.0 %copy-start.17 = (f32[384]{0:T(512)S(1)}, f32[384]{0:T(512)}, u32[]{:S(2)}) copy-start(f32[384]{0:T(512)} %param.23) | copy-start | bytes 4612
  700.2 41.1 %slice-start.5 = ((s8[18874368]{0:T(1024)(128)(4,1)}), s8[4194304]{0:T(1024)(128)(4,1)S(1)}, s32[]{:S(2)}) async-start(s8[18874368]{0:T(1024)(128)(4,1)} %bitcast.52), calls=%async_computation.6 | async-start | bytes 8388608
  704.6 36.7 %slice-start.7 = ((s8[18874368]{0:T(1024)(128)(4,1)}), s8[4194304]{0:T(1024)(128)(4,1)S(1)}, s32[]{:S(2)}) async-start(s8[18874368]{0:T(1024)(128)(4,1)} %bitcast.52), calls=%async_computation.8 | async-start | bytes 8388608
  704.6 36.7 %slice-start.8 = ((s8[18874368]{0:T(1024)(128)(4,1)}), s8[4194304]{0:T(1024)(128)(4,1)S(1)}, s32[]{:S(2)}) async-start(s8[18874368]{0:T(1024)(128)(4,1)} %bitcast.52), calls=%async_computation.9 | async-start | bytes 8388608
  704.6 36.7 %slice-start.9 = ((s8[18874368]{0:T(1024)(128)(4,1)}), s8[2097152]{0:T(1024)(128)(4,1)S(1)}, s32[]{:S(2)}) async-start(s8[18874368]{0:T(1024)(128)(4,1)} %bitcast.52), calls=%async_computation.10 | async-start | bytes 4194304
  704.7 94.3 %collective-permute-start.2 = (f32[24,57,768]{2,0,1:T(8,128)}, f32[24,57,768]{2,0,1:T(8,128)}, u32[]{:S(2)}, u32[]{:S(2)}) collective-permute-start(f32[24,57,768]{2,0,1:T(8,128)} %copy.24), channel_id=1, source_target_pairs={{8,0},{16,8},{24,16},{9,1},{17,9},{25,17},{10,2},{18,10},{26,18},{... | collective-permute-start | bytes 12607496 | tf_op jit(solution)/shard_map/ppermute | solution.py:34
  706.2 116.0 %slice-start.13 = ((s8[4718592]{0:T(1024)(128)(4,1)}), s8[4194304]{0:T(1024)(128)(4,1)S(1)}, s32[]{:S(2)}) async-start(s8[4718592]{0:T(1024)(128)(4,1)} %bitcast.56), calls=%async_computation.14 | async-start | bytes 8388608
  741.4 80.9 %slice-start.14 = ((s8[4718592]{0:T(1024)(128)(4,1)}), s8[524288]{0:T(1024)(128)(4,1)S(1)}, s32[]{:S(2)}) async-start(s8[4718592]{0:T(1024)(128)(4,1)} %bitcast.56), calls=%async_computation.15 | async-start | bytes 1048576
  816.9 140.8 %collective-permute-start.3 = (f32[24,57,768]{2,0,1:T(8,128)}, f32[24,57,768]{2,0,1:T(8,128)}, u32[]{:S(2)}, u32[]{:S(2)}) collective-permute-start(f32[24,57,768]{2,0,1:T(8,128)} %copy.26), channel_id=1, source_target_pairs={{0,8},{8,16},{16,24},{1,9},{9,17},{17,25},{2,10},{10,18},{18,26},{... | collective-permute-start | bytes 12607496 | tf_op jit(solution)/shard_map/ppermute | solution.py:34
  822.3 50.9 %slice-start.10 = ((s8[9437184]{0:T(1024)(128)(4,1)}), s8[1048576]{0:T(1024)(128)(4,1)S(1)}, s32[]{:S(2)}) async-start(s8[9437184]{0:T(1024)(128)(4,1)} %bitcast.54), calls=%async_computation.11 | async-start | bytes 2097152
  822.3 50.9 %slice-start.11 = ((s8[9437184]{0:T(1024)(128)(4,1)}), s8[4194304]{0:T(1024)(128)(4,1)S(1)}, s32[]{:S(2)}) async-start(s8[9437184]{0:T(1024)(128)(4,1)} %bitcast.54), calls=%async_computation.12 | async-start | bytes 8388608
  822.3 50.9 %slice-start.15 = ((s8[18874368]{0:T(1024)(128)(4,1)}), s8[4194304]{0:T(1024)(128)(4,1)S(1)}, s32[]{:S(2)}) async-start(s8[18874368]{0:T(1024)(128)(4,1)} %bitcast.58), calls=%async_computation.16 | async-start | bytes 8388608
  822.3 50.9 %slice-start.16 = ((s8[18874368]{0:T(1024)(128)(4,1)}), s8[4194304]{0:T(1024)(128)(4,1)S(1)}, s32[]{:S(2)}) async-start(s8[18874368]{0:T(1024)(128)(4,1)} %bitcast.58), calls=%async_computation.17 | async-start | bytes 8388608
  822.3 50.9 %slice-start.17 = ((s8[18874368]{0:T(1024)(128)(4,1)}), s8[4194304]{0:T(1024)(128)(4,1)S(1)}, s32[]{:S(2)}) async-start(s8[18874368]{0:T(1024)(128)(4,1)} %bitcast.58), calls=%async_computation.18 | async-start | bytes 8388608
  983.2 63.8 %copy-start.16 = (f32[768]{0:T(1024)S(1)}, f32[768]{0:T(1024)}, u32[]{:S(2)}) copy-start(f32[768]{0:T(1024)} %get-tuple-element.83) | copy-start | bytes 9220
  (24 other events, 477.1 us)
Sparse Core Ops, SparseCore 0:
  902.2 143.9 all-reduce.5
where the time goes:
time: 1100 us; the launch traced here: 1090 us
  matrix products  421 us (38%)
  blocking collectives  242 us (22%)
  local copies, waits for them, and re-layouts  200 us (18%)
  other arithmetic  121 us (11%)
  waiting for transfers between devices  74.6 us (7%)
  between operations  14.7 us (1%)
  starting transfers between devices  12.7 us (1%)
    dot_general x12, matrix products, tap_product(): jnp.einsum(form, left, right, precision=lax.Precision.HIGHEST, preferred_...  421 us
    scatter-add x3, local copies, waits for them, and re-layouts, on_device(): variance_gradient = variance_gradient.at[:, kernel_tap_index * DILATION_S...  102 us
    psum x2, blocking collectives, moments(): lax.psum(jnp.sum(feature_values, axis=(0, 1)), ('seq', 'dp')) / total_bins  83.1 us
    psum x2, blocking collectives, moments(): lax.psum(jnp.sum(offset * offset, axis=(0, 1)), ('seq', 'dp')) / total_bins  81.4 us
    psum x2, blocking collectives, norm_back(): lax.psum((jnp.sum(upstream, axis=(0, 1)), jnp.sum(upstream * normed, axis...  77.5 us
    ppermute x1, waiting for transfers between devices, padded(): lax.ppermute(tail, axis, [(i, (i + 1) % count) for i in range(ends)])  49.5 us
    scatter-add x2, local copies, waits for them, and re-layouts, on_device(): activation_gradient = activation_gradient.at[:, bins_per_shard - DILATION...  34.9 us
    add x1, other arithmetic, on_device(): input_grad = cotangent + input_part  25.5 us
  transfers between devices with their start and end apart: 5, of which 2 were waited for; matrix products, arithmetic and copies ran while one was open for 32% of the time, Pallas kernels for 0%

commit v1 on v0

v1 whole, which is shorter than its diff:
```python
import functools

import jax
import jax.numpy as jnp
from jax import lax
from jax.experimental import pallas as pl
from jax.experimental.pallas import tpu as pltpu
from jax.sharding import Mesh
from jax.sharding import PartitionSpec as P

STEP = 57
EDGE = 64
EPS = 1e-05
LOG2_INV_ROOT_TWO_PI = -1.3257480647361592
HALF_LOG2_E = 0.7213475204444817
MIB = 1024 * 1024
F32 = jnp.float32
BF16 = jnp.bfloat16
DP = ("chip", "core")

PHI = (
    0.7978849414599987,
    0.03633308457510501,
    -3.2594975844072696e-05,
    -5.530619400541097e-05,
    3.964744542062183e-06,
    -1.3226335479189098e-07,
    1.7561713084457843e-09,
)


def gelu_parts(v):
    square = v * v
    poly = PHI[6]
    for k in (5, 4, 3, 2, 1, 0):
        poly = poly * square + PHI[k]
    cdf = 0.5 * jnp.tanh(v * poly) + 0.5
    return v * cdf, cdf + v * jnp.exp2(square * (-HALF_LOG2_E) + LOG2_INV_ROOT_TWO_PI)


def split(v):
    high = v.astype(BF16)
    return high, (v - high.astype(F32)).astype(BF16)


def fold(x):
    return jnp.sum(x, axis=0, keepdims=True)


def dot(left, right):
    return lax.dot_general(left, right, (((1,), (0,)), ((), ())), preferred_element_type=F32)


def dot_rows(left, right):
    return lax.dot_general(left, right, (((0,), (0,)), ((), ())), preferred_element_type=F32)


def call(kernel, grid, ins, outs, scratch=(), vmem=60, flops=0, moved=0, into=(), after=(), into_first=0):
    hold = list(after) + list(into)
    aliases = {len(ins) + len(after) + k: k + into_first for k in range(len(into))}

    def body(*refs):
        kernel(*refs[: len(ins)], *refs[len(ins) + len(hold) :])

    def spec(shape, block, index, keep):
        if block is None:
            return pl.BlockSpec(shape, lambda *i: (0,) * len(shape), pipeline_mode=pl.Buffered(1) if keep else None)
        return pl.BlockSpec(block, index)

    return pl.pallas_call(
        body,
        grid=grid,
        in_specs=[spec(a.shape, b, i, True) for a, b, i in ins] + [pl.BlockSpec(memory_space=pltpu.HBM)] * len(hold),
        out_specs=[spec(s, b, i, False) for s, _, b, i in outs],
        out_shape=[jax.ShapeDtypeStruct(s, d) for s, d, _, _ in outs],
        scratch_shapes=list(scratch),
        compiler_params=pltpu.CompilerParams(vmem_limit_bytes=vmem * MIB),
        input_output_aliases=aliases,
        cost_estimate=pl.CostEstimate(flops=int(flops), bytes_accessed=int(moved), transcendentals=0),
    )(*[a for a, _, _ in ins], *hold)


def add_moments(out_ref, blocks, ref, fresh):
    windows, bins, channels = ref.shape
    rows = windows * bins

    total = eighths(ref[0])
    for w in range(1, windows):
        total = total + eighths(ref[w])
    mean = fold(total) * (1.0 / rows)
    square = None
    for w in range(windows):
        off = ref[w] - mean
        square = eighths(off * off) if square is None else square + eighths(off * off)
    square = fold(square)

    @pl.when(fresh)
    def _():
        out_ref[0:1, :] = mean
        out_ref[1:2, :] = square

    @pl.when(jnp.logical_not(fresh))
    def _():
        n = lax.convert_element_type(blocks, F32)
        share = 1.0 / (n + 1.0)
        delta = mean - out_ref[0:1, :]
        out_ref[0:1, :] = out_ref[0:1, :] + delta * share
        out_ref[1:2, :] = out_ref[1:2, :] + square + delta * delta * (rows * n * share)


def merge_moments(parts, count):
    mean = parts[0][0:1, :]
    for p in parts[1:]:
        mean = mean + p[0:1, :]
    mean = mean * (1.0 / len(parts))
    square = jnp.zeros_like(mean)
    for p in parts:
        off = p[0:1, :] - mean
        square = square + (p[1:2, :] + (off * off) * count)
    return mean, square


def merge_moments_kernel(count, *refs):
    *parts, out_ref = refs
    mean, square = merge_moments(parts, count)
    out_ref[0:1, :] = mean
    out_ref[1:2, :] = square


def peers(array, axis):
    count = lax.axis_size(axis)
    return [array] + [
        lax.ppermute(array, axis, [(i, (i + by) % count) for i in range(count)]) for by in range(1, count)
    ]


def gather_moments(moments, count):
    merged = call(
        functools.partial(merge_moments_kernel, float(count)),
        (),
        [(p, None, None) for p in peers(moments, DP)],
        [(moments.shape, F32, None, None)],
    )[0]
    return peers(merged, "seq")


def gather_sums(sums):
    return peers(functools.reduce(jnp.add, peers(sums, DP)), "seq")


def first_moments_kernel(x_ref, out_ref):
    step = pl.program_id(0)
    add_moments(out_ref, step, x_ref, step == 0)


def as_row(ref):
    return ref[...].reshape(1, ref.shape[0])


def first_finish_kernel(count, total, *refs):
    *parts, gain_ref, shift_ref, par_ref = refs
    mean, square = merge_moments(parts, count)
    inverse = lax.rsqrt(square * (1.0 / total) + EPS)
    par_ref[0:1, :] = mean
    par_ref[1:2, :] = as_row(gain_ref) * inverse
    par_ref[2:3, :] = as_row(shift_ref)
    par_ref[3:4, :] = inverse


def second_finish_kernel(count, total, *refs):
    *parts, gain_ref, shift_ref, par_ref = refs
    mean, square = merge_moments(parts, count)
    par_ref[0:1, :] = mean
    par_ref[1:2, :] = lax.rsqrt(square * (1.0 / total) + EPS)
    par_ref[2:3, :] = as_row(gain_ref)
    par_ref[3:4, :] = as_row(shift_ref)


def back_finish_kernel(total, inverse, scaled, *refs):
    *parts, par_ref, back_ref, shift_ref, gain_ref = refs
    sums = parts[0][...]
    for p in parts[1:]:
        sums = sums + p[...]
    back_ref[0:1, :] = par_ref[0:1, :]
    back_ref[1:2, :] = par_ref[inverse : inverse + 1, :]
    back_ref[2:3, :] = par_ref[1:2, :] if scaled else par_ref[2:3, :] * par_ref[inverse : inverse + 1, :]
    back_ref[3:5, :] = sums * (1.0 / total)
    shift_ref[...] = sums[0]
    gain_ref[...] = sums[1]


def put_split(ref, top, left, value):
    rows = slice(top, top + value.shape[0])
    for half, part in enumerate(split(value)):
        start = left + half * (ref.shape[1] // 2)
        ref[rows, start : start + value.shape[1]] = part


def conv_kernel(x_ref, par_ref, taps_ref, act_ref, slope_ref, mid_ref, down_ref, up_ref, w_ref, sum_ref):
    windows, bins, channels = x_ref.shape
    mid = mid_ref.shape[2]
    rows = windows * bins

    @pl.when(pl.program_id(0) == 0)
    def _():
        for t in range(3):
            put_split(w_ref, 0, t * mid, taps_ref[t])

    for w in range(windows):
        for top in range(0, bins, 32):
            own = slice(top, top + 32)
            here = (x_ref[w, own, :] - par_ref[0:1, :]) * par_ref[1:2, :] + par_ref[2:3, :]
            value, slope = gelu_parts(here)
            slope_ref[w, own, :] = slope
            high, low = split(value)
            act_ref[w, own, 0:channels] = high
            act_ref[w, own, channels:] = low
    both = dot(act_ref[:, :, 0:channels].reshape(rows, channels), w_ref[...])
    rest = dot(act_ref[:, :, channels:].reshape(rows, channels), w_ref[:, : 3 * mid])
    sum_ref[...] = both[:, : 3 * mid] + both[:, 3 * mid :] + rest
    for w in range(windows):
        top, end = w * bins, (w + 1) * bins
        mid_ref[w] = sum_ref[top:end, mid : 2 * mid]
        mid_ref[w, STEP:, :] += sum_ref[top : end - STEP, 0:mid]
        mid_ref[w, : bins - STEP, :] += sum_ref[top + STEP : end, 2 * mid :]
        down_ref[w] = sum_ref[end - EDGE : end, 0:mid]
        up_ref[w] = sum_ref[top : top + EDGE, 2 * mid :]


def point_in_kernel(cot_ref, point_ref, out_ref, w_ref):
    windows, bins, channels = cot_ref.shape
    mid = out_ref.shape[2]

    @pl.when(pl.program_id(0) == 0)
    def _():
        put_split(w_ref, 0, 0, point_ref[...].T)

    high, low = split(cot_ref[...].reshape(windows * bins, channels))
    both = dot(high, w_ref[...])
    total = both[:, :mid] + both[:, mid:] + dot(low, w_ref[:, :mid])
    out_ref[...] = total.reshape(windows, bins, mid)


def second_moments_kernel(blocks, part_ref, above_ref, below_ref, *refs):
    *before, mid_ref, out_ref = refs
    windows, bins, mid = part_ref.shape
    step = pl.program_id(0)
    lead = EDGE - STEP
    for ref in before:

        @pl.when(step == 0)
        def _(ref=ref):
            out_ref[...] = ref[...]

    for w in range(windows):
        mid_ref[w] = part_ref[w]
        mid_ref[w, 0:STEP, :] += above_ref[w, lead:, :]
        mid_ref[w, bins - STEP :, :] += below_ref[w, 0:STEP, :]
    add_moments(out_ref, step + blocks, mid_ref, step + blocks == 0)


def eighths(value):
    return jnp.sum(value.reshape(value.shape[0] // 8, 8, value.shape[1]), axis=0)


def second_act_kernel(mid_ref, g_ref, par_ref, act_ref, up_ref, sums_ref, shift_ref, gain_ref):
    windows, bins, mid = mid_ref.shape
    step = pl.program_id(0)

    @pl.when(step == 0)
    def _():
        shift_ref[...] = jnp.zeros_like(shift_ref)
        gain_ref[...] = jnp.zeros_like(gain_ref)

    shift_sum, gain_sum = shift_ref[...], gain_ref[...]
    for w in range(windows):
        for top in range(0, bins, 32):
            own = slice(top, top + 32)
            normed = (mid_ref[w, own, :] - par_ref[0:1, :]) * par_ref[1:2, :]
            value, slope = gelu_parts(normed * par_ref[2:3, :] + par_ref[3:4, :])
            up = g_ref[w, own, :] * slope
            up_ref[w, own, :] = up
            high, low = split(value)
            act_ref[w, own, 0:mid] = high
            act_ref[w, own, mid:] = low
            shift_sum = shift_sum + eighths(up)
            gain_sum = gain_sum + eighths(up * normed)
    shift_ref[...] = shift_sum
    gain_ref[...] = gain_sum

    @pl.when(step == pl.num_programs(0) - 1)
    def _():
        sums_ref[0:1, :] = fold(shift_ref[...])
        sums_ref[1:2, :] = fold(gain_ref[...])


def point_grad_kernel(cot_ref, act_ref, out_ref, sum_ref):
    windows, bins, channels = cot_ref.shape
    mid = sum_ref.shape[0]
    rows = windows * bins
    step = pl.program_id(0)

    @pl.when(step == 0)
    def _():
        sum_ref[...] = jnp.zeros_like(sum_ref)

    act = act_ref[...].reshape(rows, 2 * mid)
    high, low = split(cot_ref[...].reshape(rows, channels))
    both = dot_rows(act, high)
    sum_ref[...] += both[:mid] + both[mid:] + dot_rows(act[:, :mid], low)

    @pl.when(step == pl.num_programs(0) - 1)
    def _():
        out_ref[0] = sum_ref[...].T


def point_out_kernel(x_ref, act_ref, point_ref, out_ref, w_ref):
    windows, bins, channels = x_ref.shape
    rows, mid = windows * bins, act_ref.shape[2] // 2

    @pl.when(pl.program_id(0) == 0)
    def _():
        high, low = split(point_ref[...])
        w_ref[0:mid, :] = high
        w_ref[mid : 2 * mid, :] = high
        w_ref[2 * mid :, :] = low

    act = act_ref[...].reshape(rows, 2 * mid)
    branch = dot(act, w_ref[0 : 2 * mid, :]) + dot(act[:, :mid], w_ref[2 * mid :, :])
    out_ref[...] = x_ref[...] + branch.reshape(windows, bins, channels)


def mid_grad(up, mid, par_ref):
    normed = (mid - par_ref[0:1, :]) * par_ref[1:2, :]
    return par_ref[2:3, :] * (up - par_ref[3:4, :] - normed * par_ref[4:5, :])


def edge_grad_kernel(up_first_ref, up_last_ref, mid_first_ref, mid_last_ref, par_ref, first_ref, last_ref):
    for w in range(first_ref.shape[0]):
        first_ref[w] = mid_grad(up_first_ref[w], mid_first_ref[w], par_ref)
        last_ref[w] = mid_grad(up_last_ref[w], mid_last_ref[w], par_ref)


def widen(grad_ref, above_ref, below_ref, wide_ref, w):
    bins = grad_ref.shape[1]
    wide_ref[0:EDGE, :] = above_ref[w]
    wide_ref[EDGE : EDGE + bins, :] = grad_ref[w]
    wide_ref[EDGE + bins :, :] = below_ref[w]


def middle_grad_kernel(up_ref, mid_ref, par_ref, act_ref, grad_ref, out_ref, sum_ref, taps_ref):
    windows, bins, mid = grad_ref.shape
    rows = windows * bins
    channels = act_ref.shape[2] // 2
    step = pl.program_id(0)

    @pl.when(step == 0)
    def _():
        sum_ref[...] = jnp.zeros_like(sum_ref)

    for w in range(windows):
        for top in range(0, bins, 64):
            own = slice(top, top + 64)
            grad = mid_grad(up_ref[w, own, :], mid_ref[w, own, :], par_ref)
            grad_ref[w, own, :] = grad
            put_split(taps_ref, w * bins + top, 0, grad)
    both = dot_rows(taps_ref[...], act_ref[:, :, 0:channels].reshape(rows, channels))
    rest = dot_rows(taps_ref[:, :mid], act_ref[:, :, channels:].reshape(rows, channels))
    sum_ref[...] += both[:mid] + both[mid:] + rest

    @pl.when(step == pl.num_programs(0) - 1)
    def _():
        out_ref[0] = sum_ref[...].T


def outer_grad_kernel(first, last, grad_ref, above_ref, below_ref, act_ref, *refs):
    if not first:
        before_ref, *refs = refs
    out_ref, sum_ref, taps_ref, wide_ref = refs
    windows, bins, mid = grad_ref.shape
    count = 2 * mid
    rows = windows * bins
    channels = act_ref.shape[2] // 2
    step = pl.program_id(0)
    end = pl.num_programs(0) - (2 if last else 1)

    @pl.when(step == 0)
    def _():
        sum_ref[...] = jnp.zeros_like(sum_ref) if first else before_ref[...]

    @pl.when(step <= end)
    def _():
        for w in range(windows):
            widen(grad_ref, above_ref, below_ref, wide_ref, w)
            for k, t in enumerate((0, 2)):
                start = EDGE + (1 - t) * STEP
                put_split(taps_ref, w * bins, k * mid, wide_ref[start : start + bins, :])
        both = dot_rows(act_ref[:, :, 0:channels].reshape(rows, channels), taps_ref[...])
        rest = dot_rows(act_ref[:, :, channels:].reshape(rows, channels), taps_ref[:, :count])
        sum_ref[...] += both[:, :count] + both[:, count:] + rest

    for k in range(2 if last else 1):

        @pl.when(step == end + k)
        def _(k=k):
            if last:
                out_ref[0] = sum_ref[:, k * mid : (k + 1) * mid]
            else:
                out_ref[...] = sum_ref[...]


def act_grad_kernel(first, grad_ref, above_ref, below_ref, slope_ref, x_ref, par_ref, kernel_ref, *refs):
    if not first:
        before_ref, *refs = refs
    up_ref, sums_ref, taps_ref, part_ref, wide_ref, w_ref, sum_ref = refs
    windows, bins, mid = grad_ref.shape
    channels = x_ref.shape[2]
    depth = 3 * mid
    step = pl.program_id(0)

    @pl.when(step == 0)
    def _():
        sums_ref[...] = jnp.zeros_like(sums_ref) if first else before_ref[...]
        part_ref[...] = jnp.zeros_like(part_ref)
        for t in range(3):
            high, low = split(kernel_ref[t].T)
            own = slice(t * mid, (t + 1) * mid)
            w_ref[own, :] = high
            w_ref[depth + t * mid : depth + (t + 1) * mid, :] = high
            w_ref[2 * depth + t * mid : 2 * depth + (t + 1) * mid, :] = low

    for w in range(windows):
        widen(grad_ref, above_ref, below_ref, wide_ref, w)
        for t in range(3):
            start = EDGE + (1 - t) * STEP
            put_split(taps_ref, w * bins, t * mid, wide_ref[start : start + bins, :])
    sum_ref[...] = dot(taps_ref[...], w_ref[0 : 2 * depth, :]) + dot(taps_ref[:, :depth], w_ref[2 * depth :, :])
    shift_sum, gain_sum = part_ref[0], part_ref[1]
    for w in range(windows):
        for top in range(0, bins, 32):
            own = slice(top, top + 32)
            up = sum_ref[w * bins + top : w * bins + top + 32, :] * slope_ref[w, own, :]
            up_ref[w, own, :] = up
            shift_sum = shift_sum + eighths(up)
            gain_sum = gain_sum + eighths(up * ((x_ref[w, own, :] - par_ref[0:1, :]) * par_ref[3:4, :]))
    part_ref[0] = shift_sum
    part_ref[1] = gain_sum

    @pl.when(step == pl.num_programs(0) - 1)
    def _():
        sums_ref[0:1, :] += fold(part_ref[0])
        sums_ref[1:2, :] += fold(part_ref[1])


def input_grad_kernel(cot_ref, up_ref, x_ref, par_ref, out_ref):
    center, inverse, scale, shift_mean, gain_mean = (par_ref[k : k + 1, :] for k in range(5))
    for w in range(cot_ref.shape[0]):
        normed = (x_ref[w] - center) * inverse
        out_ref[w] = cot_ref[w] + scale * (up_ref[w] - shift_mean - normed * gain_mean)


def on_device(x, first_gain, first_shift, taps, second_gain, second_shift, point, cot):
    windows, bins, channels = x.shape
    mid = point.shape[0]
    devices = lax.axis_size("seq") * lax.axis_size(DP)
    local = windows * bins
    total = float(local * devices)
    chunks = 2 if windows % 4 == 0 else 1
    per = windows // chunks
    pair = 2 if per % 2 == 0 else 1
    quad = 4 if per % 4 == 0 else pair
    steps = per // pair
    count = per // quad
    mac = 2 * local * channels * mid

    def own(a, offset=0, size=pair, index=None):
        rest = (0,) * (a.ndim - 1)
        return (a, (size,) + a.shape[1:], index or (lambda i: (i + offset,) + rest))

    def made(shape, dtype=F32, offset=0, size=pair, index=None):
        rest = (0,) * (len(shape) - 1)
        return (shape, dtype, (size,) + shape[1:], index or (lambda i: (i + offset,) + rest))

    def whole(a):
        return (a, None, None)

    def kept(*shape, dtype=F32):
        return (shape, dtype, None, None)

    moments = call(
        first_moments_kernel,
        (windows // quad,),
        [own(x, size=quad)],
        [kept(2, channels)],
        moved=x.size * 4,
    )[0]
    gathered = gather_moments(moments, local)
    first_par = call(
        functools.partial(first_finish_kernel, float(local * lax.axis_size(DP)), total),
        (),
        [whole(p) for p in gathered] + [whole(first_gain), whole(first_shift)],
        [kept(4, channels)],
    )[0]

    seq = lax.axis_size("seq")
    onward = [(i, i + 1) for i in range(seq - 1)]
    back = [(i + 1, i) for i in range(seq - 1)]

    full, aboves, belows = (), [], []
    for c in range(chunks):
        *full, down, up = call(
            conv_kernel,
            (steps,),
            [own(x, c * steps), whole(first_par), whole(taps)],
            [
                made((windows, bins, 2 * channels), BF16, c * steps),
                made((windows, bins, channels), F32, c * steps),
                made((windows, bins, mid), F32, c * steps),
                made((per, EDGE, mid)),
                made((per, EDGE, mid)),
            ],
            [pltpu.VMEM((channels, 6 * mid), BF16), pltpu.VMEM((pair * bins, 3 * mid), F32)],
            flops=9 * mac / chunks,
            moved=x.size * 14 / chunks,
            into=full,
        )
        aboves.append(lax.ppermute(down, "seq", onward))
        belows.append(lax.ppermute(up, "seq", back))
    act, slope, partial = full

    pulled = call(
        point_in_kernel,
        (windows // quad,),
        [own(cot, size=quad), whole(point)],
        [made((windows, bins, mid), size=quad)],
        [pltpu.VMEM((channels, 2 * mid), BF16)],
        flops=3 * mac,
        moved=x.size * 6,
        after=aboves[:-1] + belows[:-1] + [partial],
    )[0]

    mids, moments = (), ()
    for c in range(chunks):
        *mids, moment = call(
            functools.partial(second_moments_kernel, c * count),
            (count,),
            [own(partial, c * count, quad), own(aboves[c], 0, quad), own(belows[c], 0, quad)] + [whole(m) for m in moments],
            [made((windows, bins, mid), F32, c * count, quad), kept(2, mid)],
            moved=x.size * 5 / chunks,
            into=mids,
            after=[pulled] if c == chunks - 1 else (),
        )
        moments = [moment]
    mids = mids[0]
    gathered = gather_moments(moment, local)
    second_par = call(
        functools.partial(second_finish_kernel, float(local * lax.axis_size(DP)), total),
        (),
        [whole(p) for p in gathered] + [whole(second_gain), whole(second_shift)],
        [kept(4, mid)],
    )[0]
    second_act, ups, sums = call(
        second_act_kernel,
        (windows // quad,),
        [own(mids, size=quad), own(pulled, size=quad), whole(second_par)],
        [made((windows, bins, 2 * mid), BF16, size=quad), made((windows, bins, mid), size=quad), kept(2, mid)],
        [pltpu.VMEM((8, mid), F32)] * 2,
        moved=x.size * 8,
    )
    gathered = gather_sums(sums)

    weight_grads = call(
        point_grad_kernel,
        (windows // quad,),
        [own(cot, size=quad), own(second_act, size=quad)],
        [made((4, channels, mid), size=1, index=lambda i: (3, 0, 0))],
        [pltpu.VMEM((mid, channels), F32)],
        flops=3 * mac,
        moved=x.size * 6,
    )

    back_par, second_shift_grad, second_gain_grad = call(
        functools.partial(back_finish_kernel, total, 1, False),
        (),
        [whole(p) for p in gathered] + [whole(second_par)],
        [kept(5, mid), kept(mid), kept(mid)],
        after=weight_grads,
    )
    grad_aboves, grad_belows = [], []
    tail = bins // EDGE - 1
    for c in range(chunks):
        edge = (quad, EDGE, mid)
        places = [lambda i, c=c, b=b: (i + c * count, b, 0) for b in (0, tail)]
        first, last = call(
            edge_grad_kernel,
            (count,),
            [(a, edge, place) for a in (ups, mids) for place in places] + [whole(back_par)],
            [made((per, EDGE, mid), size=quad), made((per, EDGE, mid), size=quad)],
            moved=x.size * 2 / chunks,
        )
        grad_aboves.append(lax.ppermute(last, "seq", onward))
        grad_belows.append(lax.ppermute(first, "seq", back))

    wide = [pltpu.VMEM((bins + 2 * EDGE, mid), F32)]
    grads, *weight_grads = call(
        middle_grad_kernel,
        (windows // quad,),
        [own(ups, size=quad), own(mids, size=quad), whole(back_par), own(act, size=quad)],
        [
            made((windows, bins, mid), size=quad),
            made((4, channels, mid), size=1, index=lambda i: (1, 0, 0)),
        ],
        [pltpu.VMEM((mid, channels), F32), pltpu.VMEM((quad * bins, 2 * mid), BF16)],
        flops=3 * mac,
        moved=x.size * 10,
        into=weight_grads,
        into_first=1,
    )
    outer = ()
    for c in range(chunks):
        end = c == chunks - 1

        def at(c=c, first=0):
            return lambda i: (jnp.minimum(i, count - 1) + first, 0, 0)

        outer = call(
            functools.partial(outer_grad_kernel, c == 0, end),
            (count + end,),
            [
                own(grads, size=quad, index=at(first=c * count)),
                own(grad_aboves[c], size=quad, index=at()),
                own(grad_belows[c], size=quad, index=at()),
                own(act, size=quad, index=at(first=c * count)),
            ]
            + [whole(o) for o in outer],
            [
                made((4, channels, mid), size=1, index=lambda i: (jnp.where(i >= count, 2, 0), 0, 0))
                if end
                else kept(channels, 2 * mid)
            ],
            [pltpu.VMEM((channels, 2 * mid), F32), pltpu.VMEM((quad * bins, 4 * mid), BF16)] + wide,
            flops=6 * mac / chunks,
            moved=x.size * 8 / chunks,
            into=weight_grads if end else (),
            after=weight_grads if c == 0 else (),
        )
    scattered = lax.psum_scatter(outer[0], DP, scatter_dimension=1, tiled=True)

    block_output = call(
        point_out_kernel,
        (windows // quad,),
        [own(x, size=quad), own(second_act, size=quad), whole(point)],
        [made((windows, bins, channels), size=quad)],
        [pltpu.VMEM((3 * mid, channels), BF16)],
        flops=3 * mac,
        moved=x.size * 10,
        after=outer[:1],
    )[0]

    sums, first_up = (), ()
    for c in range(chunks):
        *first_up, last = call(
            functools.partial(act_grad_kernel, c == 0),
            (steps,),
            [
                own(grads, c * steps),
                own(grad_aboves[c]),
                own(grad_belows[c]),
                own(slope, c * steps),
                own(x, c * steps),
                whole(first_par),
                whole(taps),
            ]
            + [whole(s) for s in sums],
            [made((windows, bins, channels), F32, c * steps), kept(2, channels)],
            [
                pltpu.VMEM((pair * bins, 6 * mid), BF16),
                pltpu.VMEM((2, 8, channels), F32),
                pltpu.VMEM((bins + 2 * EDGE, mid), F32),
                pltpu.VMEM((9 * mid, channels), BF16),
                pltpu.VMEM((pair * bins, channels), F32),
            ],
            flops=9 * mac / chunks,
            moved=x.size * 14 / chunks,
            into=first_up,
            after=[block_output] if c == 0 else (),
        )
        sums = [last]
        if c == 0:
            scattered = lax.psum(lax.optimization_barrier((scattered, last))[0], "seq")
    half_summed = functools.reduce(jnp.add, peers(last, DP))
    gathered = peers(half_summed, "seq")
    last_par, first_shift_grad, first_gain_grad = call(
        functools.partial(back_finish_kernel, total, 3, True),
        (),
        [whole(p) for p in gathered] + [whole(first_par)],
        [kept(5, channels), kept(channels), kept(channels)],
    )
    scattered = lax.optimization_barrier((scattered, half_summed))[0]
    total_grads = lax.all_gather(scattered, DP, axis=1, tiled=True)
    tap_grad = total_grads[:3]
    point_grad = total_grads[3].T
    input_grad = call(
        input_grad_kernel,
        (windows // quad,),
        [own(cot, size=quad), own(first_up[0], size=quad), own(x, size=quad), whole(last_par)],
        [made((windows, bins, channels), size=quad)],
        moved=x.size * 16,
    )[0]
    return (
        block_output,
        input_grad,
        first_gain_grad,
        first_shift_grad,
        tap_grad,
        second_gain_grad,
        second_shift_grad,
        point_grad,
    )


def solution(mesh):
    seq, dp = mesh.devices.shape
    split_mesh = Mesh(mesh.devices.reshape(seq, dp // 2, 2), ("seq",) + DP)
    rows = P(DP, "seq", None)
    return jax.shard_map(
        on_device,
        mesh=split_mesh,
        in_specs=(rows, P(), P(), P(), P(), P(), P(), rows),
        out_specs=(rows, rows, P(), P(), P(), P(), P(), P()),
        check_vma=False,
    )
```

time: 1100 us -> 456 us (0.41)
  matrix products: 421 us -> 0 us
  Pallas kernels: 0 us -> 306 us
  blocking collectives: 242 us -> 0 us
  local copies, waits for them, and re-layouts: 200 us -> 15.5 us
  other arithmetic: 121 us -> 1.4 us
  starting transfers between devices: 12.7 us -> 63.2 us
  waiting for transfers between devices: 74.6 us -> 46.1 us
    dot_general x12 -> x0, matrix products: 421 us -> none  [tap_product(): jnp.einsum(form, left, right, precision=lax.Precision.HIGHEST, preferred_...]
    pallas_call x0 -> x23, Pallas kernels: none -> 306 us  [call(): pl.pallas_call(body, grid=grid, in_specs=[spec(a.shape, b, i, True) for a...]
    psum x6 -> x0, blocking collectives: 242 us -> none  [the longest x2 83.1 us: moments(): lax.psum(jnp.sum(feature_values, axis=(0, 1)), ('seq', 'dp')) / total_bins]
    scatter-add x5 -> x0, local copies, waits for them, and re-layouts: 137 us -> none  [the longest x3 102 us: on_device(): variance_gradient = variance_gradient.at[:, kernel_tap_index * DILATION_S...]
    ppermute x4 -> x48, starting transfers between devices: 12.7 us -> 62.8 us  [the longest x40 43.6 us: peers(): lax.ppermute(array, axis, [(i, (i + by) % count) for i in range(count)])]
    reduce_sum x4 -> x0, other arithmetic: 45.8 us -> none  [the longest x1 25.3 us: norm_back(): jnp.sum(upstream, axis=(0, 1))]
    ppermute x4 -> x48, waiting for transfers between devices: 74.5 us -> 30.2 us  [the longest x40 29.4 us: peers(): lax.ppermute(array, axis, [(i, (i + by) % count) for i in range(count)])]
    slice x7 -> x1, local copies, waits for them, and re-layouts: 47.5 us -> 4.02 us  [on_device(): tap_grad = total_grads[:3]]
  transfers between devices with their start and end apart: 5 -> 51, of which waited for: 2 -> 25; matrix products, arithmetic and copies ran while one was open for 32% -> 0% of each run, Pallas kernels for 0% -> 48%
where the time goes in v1:
time: 456 us; the launch traced here: 447 us
  Pallas kernels  306 us (67%)
  starting transfers between devices  63.2 us (14%)
  waiting for transfers between devices  46.1 us (10%)
  local copies, waits for them, and re-layouts  15.5 us (3%)
  between operations  14.6 us (3%)
    pallas_call x23, Pallas kernels, call(): pl.pallas_call(body, grid=grid, in_specs=[spec(a.shape, b, i, True) for a...  306 us
    ppermute x40, starting transfers between devices, peers(): lax.ppermute(array, axis, [(i, (i + by) % count) for i in range(count)])  43.6 us
    ppermute x40, waiting for transfers between devices, peers(): lax.ppermute(array, axis, [(i, (i + by) % count) for i in range(count)])  29.4 us
    unnamed x69, local copies, waits for them, and re-layouts  10.1 us
  transfers between devices with their start and end apart: 51, of which 25 were waited for; matrix products, arithmetic and copies ran while one was open for 0% of the time, Pallas kernels for 48%

profile of v1, /device:TPU:0, one launch (start us, length us, event | category | flops | bytes accessed | tf_op | source)
XLA Modules:
  0.0 447.1 jit_solution(3214246896045999147)
XLA Ops:
  7.2 9.7 %shard_map.143.refs_0_ = f32[2,768]{1,0:T(2,128)} custom-call(f32[24,256,768]{2,1,0:T(8,128)} %refs_2_.7), custom_call_target="tpu_custom_call" | custom-call | bytes 18874368 | tf_op jit(solution)/shard_map/pallas_call | solution.py:70
  42.6 28.3 %shard_map.146 = (bf16[24,256,1536]{2,1,0:T(8,128)(2,1)}, f32[24,256,768]{2,1,0:T(8,128)}, f32[24,256,384]{2,1,0:T(8,128)}, f32[12,64,384]{2,1,0:T(8,128)}, f32[12,64,384]{2,1,0:T(8,128)}) custom-call(f32[24,256,768]{2,1,0:T(8,128)} %refs_2_.7, f32[4,768]{1,0:T(4,128)} %shard_map.145.refs_1_.refs_5_.refs_4_, f32[3,768,384]{2,1,0:T(8,128)} %refs_6_.3), custom_call_target="tpu_custom_call" | custom-call | flops 16307453952 | bytes 33030144 | tf_op jit(solution)/shard_map/pallas_call | solution.py:70
  73.6 28.6 %shard_map.147 = (bf16[24,256,1536]{2,1,0:T(8,128)(2,1)}, f32[24,256,768]{2,1,0:T(8,128)}, f32[24,256,384]{2,1,0:T(8,128)}, f32[12,64,384]{2,1,0:T(8,128)}, f32[12,64,384]{2,1,0:T(8,128)}) custom-call(f32[24,256,768]{2,1,0:T(8,128)} %refs_2_.7, ...), custom_call_target="tpu_custom_call", output_to_operand_aliasing={{0}: (3, {}), {1}: (4, {}), {2}: (5, {})} | custom-call | flops 16307453952 | bytes 33030144 | tf_op jit(solution)/shard_map/pallas_call | solution.py:70
  102.2 4.8 %collective-permute-start.10 = (f32[12,64,384]{2,1,0:T(8,128)}, f32[12,64,384]{2,1,0:T(8,128)S(1)}, u32[]{:S(2)}, u32[]{:S(2)}) collective-permute-start(f32[12,64,384]{2,1,0:T(8,128)} %get-tuple-element.47), channel_id=1, source_target_pairs={{0,8},{8,16},{16,24},{1,9},{9,17},{17,25},{2,10},{10,18},{18,26},{... | collective-permute-start | bytes 3538952 | tf_op jit(solution)/shard_map/ppermute | solution.py:527
  109.9 6.5 %shard_map.148 = (f32[24,256,384]{2,1,0:T(8,128)}, f32[2,384]{1,0:T(2,128)}) custom-call(f32[24,256,384]{2,1,0:T(8,128)} %get-tuple-element.46.refs_0_.refs_4_, f32[12,64,384]{2,1,0:T(8,128)} %copy-done, f32[12,64,384]{2,1,0:T(8,128)} %copy-done.1), custom_call_target="tpu_custom_call" | custom-call | bytes 11796480 | tf_op jit(solution)/shard_map/pallas_call | solution.py:70
  116.3 17.7 %shard_map.149.refs_4_.refs_1_ = f32[24,256,384]{2,1,0:T(8,128)} custom-call(f32[24,256,768]{2,1,0:T(8,128)} %refs_0_.13, f32[384,768]{1,0:T(8,128)} %refs_2_.6, f32[12,64,384]{2,1,0:T(8,128)} %copy-done, f32[12,64,384]{2,1,0:T(8,128)} %copy-done.1, f32[24,256,384]{2,1,0:T(8,128)} %get-tuple-element.46.refs_0_.refs_4_), custom_call_target="tpu_custom_call" | custom-call | flops 10871635968 | bytes 28311552 | tf_op jit(solution)/shard_map/pallas_call | solution.py:70
  135.0 6.5 %shard_map.150 = (f32[24,256,384]{2,1,0:T(8,128)}, f32[2,384]{1,0:T(2,128)}) custom-call(f32[24,256,384]{2,1,0:T(8,128)} %get-tuple-element.46.refs_0_.refs_4_, f32[12,64,384]{2,1,0:T(8,128)} %copy-done.4, f32[12,64,384]{2,1,0:T(8,128)} %collective-permute-done.11.refs_2_, f32[2,384]{1,0:T(2,128)} %get-tuple-element.51.refs_3_, ...), custom_call_target="tpu_custom_call", output_to_operand_aliasing={{0}: (5, {})} | custom-call | bytes 11796480 | tf_op jit(solution)/shard_map/pallas_call | solution.py:70
  153.6 4.6 %collective-permute-start.23 = (f32[2,384]{1,0:T(2,128)}, f32[2,384]{1,0:T(2,128)S(1)}, u32[]{:S(2)}, u32[]{:S(2)}) collective-permute-start(f32[2,384]{1,0:T(2,128)} %shard_map.151.refs_0_), channel_id=1, source_target_pairs={{0,24},{8,0},{16,8},{24,16},{1,25},{9,1},{17,9},{25,17},{2,26},{10... | collective-permute-start | bytes 9224 | tf_op jit(solution)/shard_map/ppermute | solution.py:133
  165.8 18.1 %shard_map.153 = (bf16[24,256,768]{2,1,0:T(8,128)(2,1)}, f32[24,256,384]{2,1,0:T(8,128)}, f32[2,384]{1,0:T(2,128)}) custom-call(f32[24,256,384]{2,1,0:T(8,128)} %get-tuple-element.53.refs_0_.refs_1_.refs_2_.refs_3_, f32[24,256,384]{2,1,0:T(8,128)} %shard_map.149.refs_4_.refs_1_, f32[4,384]{1,0:T(4,128)} %shard_map.152.refs_2_.refs_4_), custom_call_target="tpu_custom_call" | custom-call | bytes 37748736 | tf_op jit(solution)/shard_map/pallas_call | solution.py:70
  196.9 16.8 %shard_map.154.refs_5_.refs_4_ = f32[4,768,384]{2,1,0:T(8,128)} custom-call(f32[24,256,768]{2,1,0:T(8,128)} %refs_0_.13, bf16[24,256,768]{2,1,0:T(8,128)(2,1)} %get-tuple-element.55.refs_1_), custom_call_target="tpu_custom_call" | custom-call | flops 10871635968 | bytes 28311552 | tf_op jit(solution)/shard_map/pallas_call | solution.py:70
  216.3 4.6 %shard_map.158 = (f32[12,64,384]{2,1,0:T(8,128)}, f32[12,64,384]{2,1,0:T(8,128)}) custom-call(f32[24,256,384]{2,1,0:T(8,128)} %get-tuple-element.56.refs_0_.refs_1_, f32[24,256,384]{2,1,0:T(8,128)} %get-tuple-element.56.refs_0_.refs_1_, f32[24,256,384]{2,1,0:T(8,128)} %get-tuple-element.53.refs_0_.refs_1_.refs_2_.refs_3_, ...), custom_call_target="tpu_custom_call" | custom-call | bytes 4718592 | tf_op jit(solution)/shard_map/pallas_call | solution.py:70
  225.1 4.6 %shard_map.157 = (f32[12,64,384]{2,1,0:T(8,128)}, f32[12,64,384]{2,1,0:T(8,128)}) custom-call(f32[24,256,384]{2,1,0:T(8,128)} %get-tuple-element.56.refs_0_.refs_1_, f32[24,256,384]{2,1,0:T(8,128)} %get-tuple-element.56.refs_0_.refs_1_, f32[24,256,384]{2,1,0:T(8,128)} %get-tuple-element.53.refs_0_.refs_1_.refs_2_.refs_3_, ...), custom_call_target="tpu_custom_call" | custom-call | bytes 4718592 | tf_op jit(solution)/shard_map/pallas_call | solution.py:70
  229.7 4.6 %collective-permute-start.34 = (f32[12,64,384]{2,1,0:T(8,128)}, f32[12,64,384]{2,1,0:T(8,128)S(1)}, u32[]{:S(2)}, u32[]{:S(2)}) collective-permute-start(f32[12,64,384]{2,1,0:T(8,128)} %get-tuple-element.61), channel_id=1, source_target_pairs={{0,8},{8,16},{16,24},{1,9},{9,17},{17,25},{2,10},{10,18},{18,26},{... | collective-permute-start | bytes 3538952 | tf_op jit(solution)/shard_map/ppermute | solution.py:601
  235.8 21.6 %shard_map.156 = (f32[24,256,384]{2,1,0:T(8,128)}, f32[4,768,384]{2,1,0:T(8,128)}) custom-call(f32[24,256,384]{2,1,0:T(8,128)} %get-tuple-element.56.refs_0_.refs_1_, f32[24,256,384]{2,1,0:T(8,128)} %get-tuple-element.53.refs_0_.refs_1_.refs_2_.refs_3_, f32[5,384]{1,0:T(8,128)} %get-tuple-element.58.refs_2_.refs_4_, ...), custom_call_target="tpu_custom_call", output_to_operand_aliasing={{1}: (4, {})} | custom-call | flops 10871635968 | bytes 47185920 | tf_op jit(solution)/shard_map/pallas_call | solution.py:70
  258.4 17.2 %shard_map.159.refs_4_ = f32[768,768]{1,0:T(8,128)} custom-call(f32[24,256,384]{2,1,0:T(8,128)} %get-tuple-element.60.refs_0_, f32[12,64,384]{2,1,0:T(8,128)} %copy-done.5, f32[12,64,384]{2,1,0:T(8,128)} %collective-permute-done.37.refs_2_, bf16[24,256,1536]{2,1,0:T(8,128)(2,1)} %get-tuple-element.59.refs_3_, f32[4,768,384]{2,1,0:T(8,128)} %get-tuple-element.65.refs_4_.refs_5_), custom_call_target="tpu_custom_call" | custom-call | flops 10871635968 | bytes 18874368 | tf_op jit(solution)/shard_map/pallas_call | solution.py:70
  277.6 18.0 %shard_map.160.refs_3_ = f32[4,768,384]{2,1,0:T(8,128)} custom-call(f32[24,256,384]{2,1,0:T(8,128)} %get-tuple-element.60.refs_0_, f32[12,64,384]{2,1,0:T(8,128)} %copy-done.2, f32[12,64,384]{2,1,0:T(8,128)} %copy-done.3, bf16[24,256,1536]{2,1,0:T(8,128)(2,1)} %get-tuple-element.59.refs_3_, ...), custom_call_target="tpu_custom_call", output_to_operand_aliasing={{}: (5, {})} | custom-call | flops 10871635968 | bytes 18874368 | tf_op jit(solution)/shard_map/pallas_call | solution.py:70
  296.0 23.0 %shard_map.161.refs_7_ = f32[24,256,768]{2,1,0:T(8,128)} custom-call(f32[24,256,768]{2,1,0:T(8,128)} %refs_2_.7, bf16[24,256,768]{2,1,0:T(8,128)(2,1)} %get-tuple-element.55.refs_1_, f32[384,768]{1,0:T(8,128)} %refs_2_.6, f32[4,768,384]{2,1,0:T(8,128)} %shard_map.160.refs_3_), custom_call_target="tpu_custom_call" | custom-call | flops 10871635968 | bytes 47185920 | tf_op jit(solution)/shard_map/pallas_call | solution.py:70
  318.9 25.6 %shard_map.162 = (f32[24,256,768]{2,1,0:T(8,128)}, f32[2,768]{1,0:T(2,128)}) custom-call(f32[24,256,384]{2,1,0:T(8,128)} %get-tuple-element.60.refs_0_, f32[12,64,384]{2,1,0:T(8,128)} %copy-done.5, f32[12,64,384]{2,1,0:T(8,128)} %collective-permute-done.37.refs_2_, f32[24,256,768]{2,1,0:T(8,128)} %get-tuple-element.66.refs_3_, f32[24,256,768]{2,1,0:T(8,128)} %refs_2_.7, ...), custom_call_target="tpu_custom_call" | custom-call | flops 16307453952 | bytes 33030144 | tf_op jit(solution)/shard_map/pallas_call | solution.py:70
  344.5 6.4 %reduce-scatter.2.cloned.1.call-done = f32[4,96,384]{2,1,0:T(8,128)} async-done(((f32[4,768,384]{2,1,0:T(8,128)}), f32[4,96,384]{2,1,0:T(8,128)}) %reduce-scatter.2.cloned.1.call-update) | async-done | bytes 589840 | tf_op jit(solution)/shard_map/reduce_scatter | solution.py:647
  351.0 24.7 %shard_map.163 = (f32[24,256,768]{2,1,0:T(8,128)}, f32[2,768]{1,0:T(2,128)}) custom-call(f32[24,256,384]{2,1,0:T(8,128)} %get-tuple-element.60.refs_0_, f32[12,64,384]{2,1,0:T(8,128)} %copy-done.2, f32[12,64,384]{2,1,0:T(8,128)} %copy-done.3, f32[24,256,768]{2,1,0:T(8,128)} %get-tuple-element.66.refs_3_, ...), custom_call_target="tpu_custom_call", output_to_operand_aliasing={{0}: (8, {})} | custom-call | flops 16307453952 | bytes 33030144 | tf_op jit(solution)/shard_map/pallas_call | solution.py:70
  387.3 5.3 %all-reduce.2.cloned.1.call-done = f32[4,96,384]{2,1,0:T(8,128)} async-done(((f32[4,96,384]{2,1,0:T(8,128)}), f32[4,96,384]{2,1,0:T(8,128)}) %all-reduce.2.cloned.1.call-update) | async-done | bytes 589840 | tf_op jit(solution)/shard_map/psum | solution.py:690
  402.7 26.6 %shard_map.165 = f32[24,256,768]{2,1,0:T(8,128)} custom-call(f32[24,256,768]{2,1,0:T(8,128)} %refs_0_.13, f32[24,256,768]{2,1,0:T(8,128)} %get-tuple-element.69.refs_1_, f32[24,256,768]{2,1,0:T(8,128)} %refs_2_.7, f32[5,768]{1,0:T(8,128)} %get-tuple-element.71.refs_3_), custom_call_target="tpu_custom_call" | custom-call | bytes 75497472 | tf_op jit(solution)/shard_map/pallas_call | solution.py:70
  429.3 4.1 all-gather.2.cloned.1.call-done
  436.1 4.0 slice.8
  (177 shorter events, 100.7 us)
Async XLA Ops:
  7.2 343.8 %reduce-scatter.2.cloned.1.call-start = ((), (), s32[]{:S(2)}) async-start(), calls=%async_computation.1 | async-start | bytes 5308416 | tf_op jit(solution)/shard_map/reduce_scatter | solution.py:647
  16.9 5.9 %collective-permute-start.6 = (f32[2,768]{1,0:T(2,128)}, f32[2,768]{1,0:T(2,128)S(1)}, u32[]{:S(2)}, u32[]{:S(2)}) collective-permute-start(f32[2,768]{1,0:T(2,128)} %shard_map.143.refs_0_), channel_id=1, source_target_pairs={{0,7},{1,0},{2,1},{3,2},{4,3},{5,4},{6,5},{7,6},{8,15},{9,8},{10,9... | collective-permute-start | bytes 18440 | tf_op jit(solution)/shard_map/ppermute | solution.py:133
  22.8 5.2 %collective-permute-start.1 = (f32[2,768]{1,0:T(2,128)}, f32[2,768]{1,0:T(2,128)S(1)}, u32[]{:S(2)}, u32[]{:S(2)}) collective-permute-start(f32[2,768]{1,0:T(2,128)} %shard_map.143.refs_0_), channel_id=1, source_target_pairs={{0,2},{1,3},{2,4},{3,5},{4,6},{5,7},{6,0},{7,1},{8,10},{9,11},{10,... | collective-permute-start | bytes 18440 | tf_op jit(solution)/shard_map/ppermute | solution.py:133
  31.4 5.2 %collective-permute-start.9 = (f32[2,768]{1,0:T(2,128)}, f32[2,768]{1,0:T(2,128)S(1)}, u32[]{:S(2)}, u32[]{:S(2)}) collective-permute-start(f32[2,768]{1,0:T(2,128)} %shard_map.144.refs_0_), channel_id=1, source_target_pairs={{0,24},{8,0},{16,8},{24,16},{1,25},{9,1},{17,9},{25,17},{2,26},{10... | collective-permute-start | bytes 18440 | tf_op jit(solution)/shard_map/ppermute | solution.py:133
  35.0 5.6 %collective-permute-start.7 = (f32[2,768]{1,0:T(2,128)}, f32[2,768]{1,0:T(2,128)S(1)}, u32[]{:S(2)}, u32[]{:S(2)}) collective-permute-start(f32[2,768]{1,0:T(2,128)} %shard_map.144.refs_0_), channel_id=1, source_target_pairs={{0,8},{8,16},{16,24},{24,0},{1,9},{9,17},{17,25},{25,1},{2,10},{10... | collective-permute-start | bytes 18440 | tf_op jit(solution)/shard_map/ppermute | solution.py:133
  70.9 37.5 %collective-permute-start.12 = (f32[12,64,384]{2,1,0:T(8,128)}, f32[12,64,384]{2,1,0:T(8,128)S(1)}, u32[]{:S(2)}, u32[]{:S(2)}) collective-permute-start(f32[12,64,384]{2,1,0:T(8,128)} %get-tuple-element.49), channel_id=1, source_target_pairs={{0,8},{8,16},{16,24},{1,9},{9,17},{17,25},{2,10},{10,18},{18,26},{... | collective-permute-start | bytes 3538952 | tf_op jit(solution)/shard_map/ppermute | solution.py:527
  72.3 36.2 %collective-permute-start.13 = (f32[12,64,384]{2,1,0:T(8,128)}, f32[12,64,384]{2,1,0:T(8,128)S(1)}, u32[]{:S(2)}, u32[]{:S(2)}) collective-permute-start(f32[12,64,384]{2,1,0:T(8,128)} %get-tuple-element.50), channel_id=1, source_target_pairs={{8,0},{16,8},{24,16},{9,1},{17,9},{25,17},{10,2},{18,10},{26,18},{... | collective-permute-start | bytes 3538952 | tf_op jit(solution)/shard_map/ppermute | solution.py:528
  102.2 31.9 %collective-permute-start.10 = (f32[12,64,384]{2,1,0:T(8,128)}, f32[12,64,384]{2,1,0:T(8,128)S(1)}, u32[]{:S(2)}, u32[]{:S(2)}) collective-permute-start(f32[12,64,384]{2,1,0:T(8,128)} %get-tuple-element.47), channel_id=1, source_target_pairs={{0,8},{8,16},{16,24},{1,9},{9,17},{17,25},{2,10},{10,18},{18,26},{... | collective-permute-start | bytes 3538952 | tf_op jit(solution)/shard_map/ppermute | solution.py:527
  107.0 27.1 %collective-permute-start.11 = (f32[12,64,384]{2,1,0:T(8,128)}, f32[12,64,384]{2,1,0:T(8,128)}, u32[]{:S(2)}, u32[]{:S(2)}) collective-permute-start(f32[12,64,384]{2,1,0:T(8,128)} %get-tuple-element.48), channel_id=1, source_target_pairs={{8,0},{16,8},{24,16},{9,1},{17,9},{25,17},{10,2},{18,10},{26,18},{... | collective-permute-start | bytes 3538952 | tf_op jit(solution)/shard_map/ppermute | solution.py:528
  141.6 6.0 %collective-permute-start.19 = (f32[2,384]{1,0:T(2,128)}, f32[2,384]{1,0:T(2,128)S(1)}, u32[]{:S(2)}, u32[]{:S(2)}) collective-permute-start(f32[2,384]{1,0:T(2,128)} %get-tuple-element.54.refs_0_), channel_id=1, source_target_pairs={{0,6},{1,7},{2,0},{3,1},{4,2},{5,3},{6,4},{7,5},{8,14},{9,15},{10,... | collective-permute-start | bytes 9224 | tf_op jit(solution)/shard_map/ppermute | solution.py:133
  153.6 6.1 %collective-permute-start.23 = (f32[2,384]{1,0:T(2,128)}, f32[2,384]{1,0:T(2,128)S(1)}, u32[]{:S(2)}, u32[]{:S(2)}) collective-permute-start(f32[2,384]{1,0:T(2,128)} %shard_map.151.refs_0_), channel_id=1, source_target_pairs={{0,24},{8,0},{16,8},{24,16},{1,25},{9,1},{17,9},{25,17},{2,26},{10... | collective-permute-start | bytes 9224 | tf_op jit(solution)/shard_map/ppermute | solution.py:133
  158.2 5.6 %collective-permute-start.21 = (f32[2,384]{1,0:T(2,128)}, f32[2,384]{1,0:T(2,128)S(1)}, u32[]{:S(2)}, u32[]{:S(2)}) collective-permute-start(f32[2,384]{1,0:T(2,128)} %shard_map.151.refs_0_), channel_id=1, source_target_pairs={{0,8},{8,16},{16,24},{24,0},{1,9},{9,17},{17,25},{25,1},{2,10},{10... | collective-permute-start | bytes 9224 | tf_op jit(solution)/shard_map/ppermute | solution.py:133
  183.9 4.9 %collective-permute-start.29 = (f32[2,384]{1,0:T(2,128)}, f32[2,384]{1,0:T(2,128)S(1)}, u32[]{:S(2)}, u32[]{:S(2)}) collective-permute-start(f32[2,384]{1,0:T(2,128)} %get-tuple-element.57), channel_id=1, source_target_pairs={{0,6},{1,7},{2,0},{3,1},{4,2},{5,3},{6,4},{7,5},{8,14},{9,15},{10,... | collective-permute-start | bytes 9224 | tf_op jit(solution)/shard_map/ppermute | solution.py:133
  193.7 20.0 %collective-permute-start.33 = (f32[2,384]{1,0:T(2,128)S(1)}, f32[2,384]{1,0:T(2,128)S(1)}, u32[]{:S(2)}, u32[]{:S(2)}) collective-permute-start(f32[2,384]{1,0:T(2,128)S(1)} %add_add_fusion.1.refs_0_), channel_id=1, source_target_pairs={{0,24},{8,0},{16,8},{24,16},{1,25},{9,1},{17,9},{25,17},{2,26},{10... | collective-permute-start | bytes 9224 | tf_op jit(solution)/shard_map/ppermute | solution.py:133
  194.4 19.4 %collective-permute-start.32 = (f32[2,384]{1,0:T(2,128)S(1)}, f32[2,384]{1,0:T(2,128)S(1)}, u32[]{:S(2)}, u32[]{:S(2)}) collective-permute-start(f32[2,384]{1,0:T(2,128)S(1)} %add_add_fusion.1.refs_0_), channel_id=1, source_target_pairs={{0,16},{8,24},{16,0},{24,8},{1,17},{9,25},{17,1},{25,9},{2,18},{10... | collective-permute-start | bytes 9224 | tf_op jit(solution)/shard_map/ppermute | solution.py:133
  195.0 18.8 %collective-permute-start.31 = (f32[2,384]{1,0:T(2,128)S(1)}, f32[2,384]{1,0:T(2,128)S(1)}, u32[]{:S(2)}, u32[]{:S(2)}) collective-permute-start(f32[2,384]{1,0:T(2,128)S(1)} %add_add_fusion.1.refs_0_), channel_id=1, source_target_pairs={{0,8},{8,16},{16,24},{24,0},{1,9},{9,17},{17,25},{25,1},{2,10},{10... | collective-permute-start | bytes 9224 | tf_op jit(solution)/shard_map/ppermute | solution.py:133
  220.9 36.5 %collective-permute-start.36 = (f32[12,64,384]{2,1,0:T(8,128)}, f32[12,64,384]{2,1,0:T(8,128)S(1)}, u32[]{:S(2)}, u32[]{:S(2)}) collective-permute-start(f32[12,64,384]{2,1,0:T(8,128)} %get-tuple-element.63), channel_id=1, source_target_pairs={{0,8},{8,16},{16,24},{1,9},{9,17},{17,25},{2,10},{10,18},{18,26},{... | collective-permute-start | bytes 3538952 | tf_op jit(solution)/shard_map/ppermute | solution.py:601
  223.8 33.6 %collective-permute-start.37 = (f32[12,64,384]{2,1,0:T(8,128)}, f32[12,64,384]{2,1,0:T(8,128)}, u32[]{:S(2)}, u32[]{:S(2)}) collective-permute-start(f32[12,64,384]{2,1,0:T(8,128)} %get-tuple-element.64), channel_id=1, source_target_pairs={{8,0},{16,8},{24,16},{9,1},{17,9},{25,17},{10,2},{18,10},{26,18},{... | collective-permute-start | bytes 3538952 | tf_op jit(solution)/shard_map/ppermute | solution.py:602
  229.7 45.9 %collective-permute-start.34 = (f32[12,64,384]{2,1,0:T(8,128)}, f32[12,64,384]{2,1,0:T(8,128)S(1)}, u32[]{:S(2)}, u32[]{:S(2)}) collective-permute-start(f32[12,64,384]{2,1,0:T(8,128)} %get-tuple-element.61), channel_id=1, source_target_pairs={{0,8},{8,16},{16,24},{1,9},{9,17},{17,25},{2,10},{10,18},{18,26},{... | collective-permute-start | bytes 3538952 | tf_op jit(solution)/shard_map/ppermute | solution.py:601
  234.3 42.1 %collective-permute-start.35 = (f32[12,64,384]{2,1,0:T(8,128)}, f32[12,64,384]{2,1,0:T(8,128)S(1)}, u32[]{:S(2)}, u32[]{:S(2)}) collective-permute-start(f32[12,64,384]{2,1,0:T(8,128)} %get-tuple-element.62), channel_id=1, source_target_pairs={{8,0},{16,8},{24,16},{9,1},{17,9},{25,17},{10,2},{18,10},{26,18},{... | collective-permute-start | bytes 3538952 | tf_op jit(solution)/shard_map/ppermute | solution.py:602
  295.6 97.0 %all-reduce.2.cloned.1.call-start = ((), (), s32[]{:S(2)}) async-start(), calls=%async_computation.2 | async-start | bytes 1179648 | tf_op jit(solution)/shard_map/psum | solution.py:690
  351.0 82.4 %all-gather.2.cloned.1.call-start = ((), (), s32[]{:S(2)}) async-start(), calls=%async_computation.3 | async-start | bytes 5308416 | tf_op jit(solution)/shard_map/all_gather | solution.py:700
  376.6 5.8 %collective-permute-start.43 = (f32[2,768]{1,0:T(2,128)}, f32[2,768]{1,0:T(2,128)S(1)}, u32[]{:S(2)}, u32[]{:S(2)}) collective-permute-start(f32[2,768]{1,0:T(2,128)} %get-tuple-element.70), channel_id=1, source_target_pairs={{0,6},{1,7},{2,0},{3,1},{4,2},{5,3},{6,4},{7,5},{8,14},{9,15},{10,... | collective-permute-start | bytes 18440 | tf_op jit(solution)/shard_map/ppermute | solution.py:133
  395.3 5.4 %collective-permute-start.45 = (f32[2,768]{1,0:T(2,128)S(1)}, f32[2,768]{1,0:T(2,128)S(1)}, u32[]{:S(2)}, u32[]{:S(2)}) collective-permute-start(f32[2,768]{1,0:T(2,128)S(1)} %add_add_fusion.refs_0_), channel_id=1, source_target_pairs={{0,8},{8,16},{16,24},{24,0},{1,9},{9,17},{17,25},{25,1},{2,10},{10... | collective-permute-start | bytes 18440 | tf_op jit(solution)/shard_map/ppermute | solution.py:133
  (61 other events, 221.3 us)
Sparse Core Ops, SparseCore 0:
  295.8 55.1 reduce-scatter.1
  353.4 39.2 all-reduce.1
  394.7 38.5 all-gather.1

commit v2 on v1

--- a/solution.py
+++ b/solution.py
@@ -55,9 +55,9 @@
     return lax.dot_general(left, right, (((0,), (0,)), ((), ())), preferred_element_type=F32)
 
 
-def call(kernel, grid, ins, outs, scratch=(), vmem=60, flops=0, moved=0, into=(), after=(), into_first=0):
+def call(kernel, grid, ins, outs, scratch=(), vmem=60, flops=0, moved=0, into=(), after=()):
     hold = list(after) + list(into)
-    aliases = {len(ins) + len(after) + k: k + into_first for k in range(len(into))}
+    aliases = {len(ins) + len(after) + k: k for k in range(len(into))}
 
     def body(*refs):
         kernel(*refs[: len(ins)], *refs[len(ins) + len(hold) :])
@@ -157,7 +157,7 @@
     return ref[...].reshape(1, ref.shape[0])
 
 
-def first_finish_kernel(count, total, *refs):
+def first_finish(count, total, *refs):
     *parts, gain_ref, shift_ref, par_ref = refs
     mean, square = merge_moments(parts, count)
     inverse = lax.rsqrt(square * (1.0 / total) + EPS)
@@ -167,7 +167,7 @@
     par_ref[3:4, :] = inverse
 
 
-def second_finish_kernel(count, total, *refs):
+def second_finish(count, total, *refs):
     *parts, gain_ref, shift_ref, par_ref = refs
     mean, square = merge_moments(parts, count)
     par_ref[0:1, :] = mean
@@ -176,7 +176,7 @@
     par_ref[3:4, :] = as_row(shift_ref)
 
 
-def back_finish_kernel(total, inverse, scaled, *refs):
+def back_finish(total, inverse, scaled, *refs):
     *parts, par_ref, back_ref, shift_ref, gain_ref = refs
     sums = parts[0][...]
     for p in parts[1:]:
@@ -196,13 +196,20 @@
         ref[rows, start : start + value.shape[1]] = part
 
 
-def conv_kernel(x_ref, par_ref, taps_ref, act_ref, slope_ref, mid_ref, down_ref, up_ref, w_ref, sum_ref):
+def conv_kernel(finish, x_ref, taps_ref, *refs):
+    if finish is None:
+        par_ref, *refs = refs
+        act_ref, slope_ref, mid_ref, down_ref, up_ref, w_ref, sum_ref = refs
+    else:
+        *raw, act_ref, slope_ref, mid_ref, down_ref, up_ref, par_ref, w_ref, sum_ref = refs
     windows, bins, channels = x_ref.shape
     mid = mid_ref.shape[2]
     rows = windows * bins
 
     @pl.when(pl.program_id(0) == 0)
     def _():
+        if finish is not None:
+            finish(*raw, par_ref)
         for t in range(3):
             put_split(w_ref, 0, t * mid, taps_ref[t])
 
@@ -263,12 +270,21 @@
     return jnp.sum(value.reshape(value.shape[0] // 8, 8, value.shape[1]), axis=0)
 
 
-def second_act_kernel(mid_ref, g_ref, par_ref, act_ref, up_ref, sums_ref, shift_ref, gain_ref):
+def point_in_moments_kernel(
+    cot_ref, point_ref, part_ref, above_ref, below_ref, out_ref, mid_ref, moments_ref, w_ref
+):
+    point_in_kernel(cot_ref, point_ref, out_ref, w_ref)
+    second_moments_kernel(0, part_ref, above_ref, below_ref, mid_ref, moments_ref)
+
+
+def second_act_kernel(finish, mid_ref, g_ref, *refs):
+    *raw, act_ref, up_ref, sums_ref, par_ref, shift_ref, gain_ref = refs
     windows, bins, mid = mid_ref.shape
     step = pl.program_id(0)
 
     @pl.when(step == 0)
     def _():
+        finish(*raw, par_ref)
         shift_ref[...] = jnp.zeros_like(shift_ref)
         gain_ref[...] = jnp.zeros_like(gain_ref)
 
@@ -335,7 +351,16 @@
     return par_ref[2:3, :] * (up - par_ref[3:4, :] - normed * par_ref[4:5, :])
 
 
-def edge_grad_kernel(up_first_ref, up_last_ref, mid_first_ref, mid_last_ref, par_ref, first_ref, last_ref):
+def edge_grad_kernel(finish, up_first_ref, up_last_ref, mid_first_ref, mid_last_ref, *refs):
+    if finish is None:
+        par_ref, first_ref, last_ref = refs
+    else:
+        *raw, first_ref, last_ref, par_ref, shift_ref, gain_ref = refs
+
+        @pl.when(pl.program_id(0) == 0)
+        def _():
+            finish(*raw, par_ref, shift_ref, gain_ref)
+
     for w in range(first_ref.shape[0]):
         first_ref[w] = mid_grad(up_first_ref[w], mid_first_ref[w], par_ref)
         last_ref[w] = mid_grad(up_last_ref[w], mid_last_ref[w], par_ref)
@@ -452,7 +477,13 @@
         sums_ref[1:2, :] += fold(part_ref[1])
 
 
-def input_grad_kernel(cot_ref, up_ref, x_ref, par_ref, out_ref):
+def input_grad_kernel(finish, cot_ref, up_ref, x_ref, *refs):
+    *raw, out_ref, shift_ref, gain_ref, par_ref = refs
+
+    @pl.when(pl.program_id(0) == 0)
+    def _():
+        finish(*raw, par_ref, shift_ref, gain_ref)
+
     center, inverse, scale, shift_mean, gain_mean = (par_ref[k : k + 1, :] for k in range(5))
     for w in range(cot_ref.shape[0]):
         normed = (x_ref[w] - center) * inverse
@@ -495,12 +526,8 @@
         moved=x.size * 4,
     )[0]
     gathered = gather_moments(moments, local)
-    first_par = call(
-        functools.partial(first_finish_kernel, float(local * lax.axis_size(DP)), total),
-        (),
-        [whole(p) for p in gathered] + [whole(first_gain), whole(first_shift)],
-        [kept(4, channels)],
-    )[0]
+    first_finish_here = functools.partial(first_finish, float(local * lax.axis_size(DP)), total)
+    first_raw = [whole(p) for p in gathered] + [whole(first_gain), whole(first_shift)]
 
     seq = lax.axis_size("seq")
     onward = [(i, i + 1) for i in range(seq - 1)]
@@ -509,61 +536,67 @@
     full, aboves, belows = (), [], []
     for c in range(chunks):
         *full, down, up = call(
-            conv_kernel,
+            functools.partial(conv_kernel, None if c else first_finish_here),
             (steps,),
-            [own(x, c * steps), whole(first_par), whole(taps)],
+            [own(x, c * steps), whole(taps)] + ([whole(first_par)] if c else first_raw),
             [
                 made((windows, bins, 2 * channels), BF16, c * steps),
                 made((windows, bins, channels), F32, c * steps),
                 made((windows, bins, mid), F32, c * steps),
                 made((per, EDGE, mid)),
                 made((per, EDGE, mid)),
-            ],
+            ]
+            + ([] if c else [kept(4, channels)]),
             [pltpu.VMEM((channels, 6 * mid), BF16), pltpu.VMEM((pair * bins, 3 * mid), F32)],
             flops=9 * mac / chunks,
             moved=x.size * 14 / chunks,
             into=full,
         )
+        if c == 0:
+            down, up, first_par = full[3], down, up
+            full = full[:3]
         aboves.append(lax.ppermute(down, "seq", onward))
         belows.append(lax.ppermute(up, "seq", back))
     act, slope, partial = full
 
-    pulled = call(
-        point_in_kernel,
-        (windows // quad,),
-        [own(cot, size=quad), whole(point)],
-        [made((windows, bins, mid), size=quad)],
+    first_steps = windows // quad
+    small = per // first_steps if per % first_steps == 0 else per
+    pulled, mids, moment = call(
+        point_in_moments_kernel,
+        (first_steps,),
+        [
+            own(cot, size=quad),
+            whole(point),
+            own(partial, size=small),
+            own(aboves[0], size=small),
+            own(belows[0], size=small),
+        ],
+        [made((windows, bins, mid), size=quad), made((windows, bins, mid), size=small), kept(2, mid)],
         [pltpu.VMEM((channels, 2 * mid), BF16)],
         flops=3 * mac,
-        moved=x.size * 6,
-        after=aboves[:-1] + belows[:-1] + [partial],
-    )[0]
-
-    mids, moments = (), ()
-    for c in range(chunks):
+        moved=x.size * 8,
+    )
+
+    mids = [mids]
+    for c in range(1, chunks):
         *mids, moment = call(
             functools.partial(second_moments_kernel, c * count),
             (count,),
-            [own(partial, c * count, quad), own(aboves[c], 0, quad), own(belows[c], 0, quad)] + [whole(m) for m in moments],
+            [own(partial, c * count, quad), own(aboves[c], 0, quad), own(belows[c], 0, quad), whole(moment)],
             [made((windows, bins, mid), F32, c * count, quad), kept(2, mid)],
             moved=x.size * 5 / chunks,
             into=mids,
-            after=[pulled] if c == chunks - 1 else (),
+            after=[pulled],
         )
-        moments = [moment]
     mids = mids[0]
     gathered = gather_moments(moment, local)
-    second_par = call(
-        functools.partial(second_finish_kernel, float(local * lax.axis_size(DP)), total),
-        (),
-        [whole(p) for p in gathered] + [whole(second_gain), whole(second_shift)],
-        [kept(4, mid)],
-    )[0]
-    second_act, ups, sums = call(
-        second_act_kernel,
+    second_finish_here = functools.partial(second_finish, float(local * lax.axis_size(DP)), total)
+    second_raw = [whole(p) for p in gathered] + [whole(second_gain), whole(second_shift)]
+    second_act, ups, sums, second_par = call(
+        functools.partial(second_act_kernel, second_finish_here),
         (windows // quad,),
-        [own(mids, size=quad), own(pulled, size=quad), whole(second_par)],
-        [made((windows, bins, 2 * mid), BF16, size=quad), made((windows, bins, mid), size=quad), kept(2, mid)],
+        [own(mids, size=quad), own(pulled, size=quad)] + second_raw,
+        [made((windows, bins, 2 * mid), BF16, size=quad), made((windows, bins, mid), size=quad), kept(2, mid), kept(4, mid)],
         [pltpu.VMEM((8, mid), F32)] * 2,
         moved=x.size * 8,
     )
@@ -573,48 +606,48 @@
         point_grad_kernel,
         (windows // quad,),
         [own(cot, size=quad), own(second_act, size=quad)],
-        [made((4, channels, mid), size=1, index=lambda i: (3, 0, 0))],
+        [kept(1, channels, mid)],
         [pltpu.VMEM((mid, channels), F32)],
         flops=3 * mac,
         moved=x.size * 6,
     )
 
-    back_par, second_shift_grad, second_gain_grad = call(
-        functools.partial(back_finish_kernel, total, 1, False),
-        (),
-        [whole(p) for p in gathered] + [whole(second_par)],
-        [kept(5, mid), kept(mid), kept(mid)],
-        after=weight_grads,
-    )
+    early = lax.psum_scatter(weight_grads[0], DP, scatter_dimension=1, tiled=True)
+
+    back_finish_here = functools.partial(back_finish, total, 1, False)
+    back_raw = [whole(p) for p in gathered] + [whole(second_par)]
     grad_aboves, grad_belows = [], []
     tail = bins // EDGE - 1
     for c in range(chunks):
         edge = (quad, EDGE, mid)
         places = [lambda i, c=c, b=b: (i + c * count, b, 0) for b in (0, tail)]
-        first, last = call(
-            edge_grad_kernel,
+        first, last, *more = call(
+            functools.partial(edge_grad_kernel, None if c else back_finish_here),
             (count,),
-            [(a, edge, place) for a in (ups, mids) for place in places] + [whole(back_par)],
-            [made((per, EDGE, mid), size=quad), made((per, EDGE, mid), size=quad)],
+            [(a, edge, place) for a in (ups, mids) for place in places] + ([whole(back_par)] if c else back_raw),
+            [made((per, EDGE, mid), size=quad), made((per, EDGE, mid), size=quad)]
+            + ([] if c else [kept(5, mid), kept(mid), kept(mid)]),
             moved=x.size * 2 / chunks,
+            after=() if c else weight_grads,
         )
+        if c == 0:
+            back_par, second_shift_grad, second_gain_grad = more
         grad_aboves.append(lax.ppermute(last, "seq", onward))
         grad_belows.append(lax.ppermute(first, "seq", back))
 
     wide = [pltpu.VMEM((bins + 2 * EDGE, mid), F32)]
-    grads, *weight_grads = call(
+    grads, *tap_grads = call(
         middle_grad_kernel,
         (windows // quad,),
         [own(ups, size=quad), own(mids, size=quad), whole(back_par), own(act, size=quad)],
         [
             made((windows, bins, mid), size=quad),
-            made((4, channels, mid), size=1, index=lambda i: (1, 0, 0)),
+            made((3, channels, mid), size=1, index=lambda i: (1, 0, 0)),
         ],
         [pltpu.VMEM((mid, channels), F32), pltpu.VMEM((quad * bins, 2 * mid), BF16)],
         flops=3 * mac,
         moved=x.size * 10,
-        into=weight_grads,
-        into_first=1,
+        after=[first, last],
     )
     outer = ()
     for c in range(chunks):
@@ -634,17 +667,19 @@
             ]
             + [whole(o) for o in outer],
             [
-                made((4, channels, mid), size=1, index=lambda i: (jnp.where(i >= count, 2, 0), 0, 0))
+                made((3, channels, mid), size=1, index=lambda i: (jnp.where(i >= count, 2, 0), 0, 0))
                 if end
                 else kept(channels, 2 * mid)
             ],
             [pltpu.VMEM((channels, 2 * mid), F32), pltpu.VMEM((quad * bins, 4 * mid), BF16)] + wide,
             flops=6 * mac / chunks,
             moved=x.size * 8 / chunks,
-            into=weight_grads if end else (),
-            after=weight_grads if c == 0 else (),
+            into=tap_grads if end else (),
+            after=tap_grads if c == 0 else (),
         )
-    scattered = lax.psum_scatter(outer[0], DP, scatter_dimension=1, tiled=True)
+    late = lax.optimization_barrier((outer[0], early))[0]
+    late = lax.psum_scatter(late, DP, scatter_dimension=1, tiled=True)
+    scattered = jnp.concatenate([late, early], axis=0)
 
     block_output = call(
         point_out_kernel,
@@ -690,23 +725,20 @@
             scattered = lax.psum(lax.optimization_barrier((scattered, last))[0], "seq")
     half_summed = functools.reduce(jnp.add, peers(last, DP))
     gathered = peers(half_summed, "seq")
-    last_par, first_shift_grad, first_gain_grad = call(
-        functools.partial(back_finish_kernel, total, 3, True),
-        (),
-        [whole(p) for p in gathered] + [whole(first_par)],
-        [kept(5, channels), kept(channels), kept(channels)],
-    )
     scattered = lax.optimization_barrier((scattered, half_summed))[0]
     total_grads = lax.all_gather(scattered, DP, axis=1, tiled=True)
     tap_grad = total_grads[:3]
     point_grad = total_grads[3].T
-    input_grad = call(
-        input_grad_kernel,
+    input_grad, first_shift_grad, first_gain_grad = call(
+        functools.partial(input_grad_kernel, functools.partial(back_finish, total, 3, True)),
         (windows // quad,),
-        [own(cot, size=quad), own(first_up[0], size=quad), own(x, size=quad), whole(last_par)],
-        [made((windows, bins, channels), size=quad)],
+        [own(cot, size=quad), own(first_up[0], size=quad), own(x, size=quad)]
+        + [whole(p) for p in gathered]
+        + [whole(first_par)],
+        [made((windows, bins, channels), size=quad), kept(channels), kept(channels)],
+        [pltpu.VMEM((5, channels), F32)],
         moved=x.size * 16,
-    )[0]
+    )
     return (
         block_output,
         input_grad,

time: 456 us -> 442 us (0.969)
  Pallas kernels: 306 us -> 297 us
    pallas_call x23 -> x18, Pallas kernels: 306 us -> 297 us  [call(): pl.pallas_call(body, grid=grid, in_specs=[spec(a.shape, b, i, True) for a...]
    reduce_scatter x1 -> x2, waiting for transfers between devices: 6.39 us -> 0.01 us  [the longest x1 0.01 us: on_device(): lax.psum_scatter(weight_grads[0], DP, scatter_dimension=1, tiled=True)]
    unnamed x69 -> x71, local copies, waits for them, and re-layouts: 10.1 us -> 10.1 us
  transfers between devices with their start and end apart: 51 -> 52, of which waited for: 25 -> 22; matrix products, arithmetic and copies ran while one was open for 0% -> 0% of each run, Pallas kernels for 48% -> 52%
where the time goes in v2:
time: 442 us; the launch traced here: 434 us
  Pallas kernels  297 us (67%)
  starting transfers between devices  61.4 us (14%)
  waiting for transfers between devices  42.5 us (10%)
  local copies, waits for them, and re-layouts  15.4 us (3%)
  between operations  14.6 us (3%)
    pallas_call x18, Pallas kernels, call(): pl.pallas_call(body, grid=grid, in_specs=[spec(a.shape, b, i, True) for a...  297 us
    ppermute x40, starting transfers between devices, peers(): lax.ppermute(array, axis, [(i, (i + by) % count) for i in range(count)])  40.4 us
    ppermute x40, waiting for transfers between devices, peers(): lax.ppermute(array, axis, [(i, (i + by) % count) for i in range(count)])  29.4 us
    unnamed x71, local copies, waits for them, and re-layouts  10.1 us
    ppermute x2, starting transfers between devices, on_device(): grad_aboves.append(lax.ppermute(last, 'seq', onward))  9.05 us
  transfers between devices with their start and end apart: 52, of which 22 were waited for; matrix products, arithmetic and copies ran while one was open for 0% of the time, Pallas kernels for 52%

profile of v2, /device:TPU:0, one launch (start us, length us, event | category | flops | bytes accessed | tf_op | source)
XLA Modules:
  0.0 433.9 jit_solution(10032887326654976564)
XLA Ops:
  7.2 9.7 %shard_map.143.refs_0_ = f32[2,768]{1,0:T(2,128)} custom-call(f32[24,256,768]{2,1,0:T(8,128)} %refs_2_.3), custom_call_target="tpu_custom_call" | custom-call | bytes 18874368 | tf_op jit(solution)/shard_map/pallas_call | solution.py:70
  31.4 3.6 collective-permute-start.9
  41.2 28.6 %shard_map.145 = (bf16[24,256,1536]{2,1,0:T(8,128)(2,1)}, f32[24,256,768]{2,1,0:T(8,128)}, f32[24,256,384]{2,1,0:T(8,128)}, f32[12,64,384]{2,1,0:T(8,128)}, f32[12,64,384]{2,1,0:T(8,128)}, /*index=5*/f32[4,768]{1,0:T(4,128)}) custom-call(f32[24,256,768]{2,1,0:T(8,128)} %refs_2_.3, f32[3,768,384]{2,1,0:T(8,128)} %refs_6_.7, f32[2,768]{1,0:T(2,128)} %shard_map.144.refs_2_, ...), custom_call_target="tpu_custom_call" | custom-call | flops 16307453952 | bytes 33030144 | tf_op jit(solution)/shard_map/pallas_call | solution.py:70
  72.5 28.5 %shard_map.146 = (bf16[24,256,1536]{2,1,0:T(8,128)(2,1)}, f32[24,256,768]{2,1,0:T(8,128)}, f32[24,256,384]{2,1,0:T(8,128)}, f32[12,64,384]{2,1,0:T(8,128)}, f32[12,64,384]{2,1,0:T(8,128)}) custom-call(f32[24,256,768]{2,1,0:T(8,128)} %refs_2_.3, f32[3,768,384]{2,1,0:T(8,128)} %refs_6_.7, ...), custom_call_target="tpu_custom_call", output_to_operand_aliasing={{0}: (3, {}), {1}: (4, {}), {2}: (5, {})} | custom-call | flops 16307453952 | bytes 33030144 | tf_op jit(solution)/shard_map/pallas_call | solution.py:70
  101.0 4.8 %collective-permute-start.10 = (f32[12,64,384]{2,1,0:T(8,128)}, f32[12,64,384]{2,1,0:T(8,128)S(1)}, u32[]{:S(2)}, u32[]{:S(2)}) collective-permute-start(f32[12,64,384]{2,1,0:T(8,128)} %get-tuple-element.52), channel_id=1, source_target_pairs={{0,8},{8,16},{16,24},{1,9},{9,17},{17,25},{2,10},{10,18},{18,26},{... | collective-permute-start | bytes 3538952 | tf_op jit(solution)/shard_map/ppermute | solution.py:558
  108.4 20.4 %shard_map.147 = (f32[24,256,384]{2,1,0:T(8,128)}, f32[24,256,384]{2,1,0:T(8,128)}, f32[2,384]{1,0:T(2,128)}) custom-call(f32[24,256,768]{2,1,0:T(8,128)} %refs_0_.13, f32[384,768]{1,0:T(8,128)} %refs_2_.2, f32[24,256,384]{2,1,0:T(8,128)} %get-tuple-element.51.refs_2_.refs_0_, f32[12,64,384]{2,1,0:T(8,128)} %copy-done.31, ...), custom_call_target="tpu_custom_call" | custom-call | flops 10871635968 | bytes 37748736 | tf_op jit(solution)/shard_map/pallas_call | solution.py:70
  128.8 3.8 collective-permute-done.11.refs_2_
  133.6 6.6 %shard_map.148 = (f32[24,256,384]{2,1,0:T(8,128)}, f32[2,384]{1,0:T(2,128)}) custom-call(f32[24,256,384]{2,1,0:T(8,128)} %get-tuple-element.51.refs_2_.refs_0_, f32[12,64,384]{2,1,0:T(8,128)} %copy-done, f32[12,64,384]{2,1,0:T(8,128)} %copy-done.1, f32[2,384]{1,0:T(2,128)} %get-tuple-element.56.refs_3_, ...), custom_call_target="tpu_custom_call", output_to_operand_aliasing={{0}: (5, {})} | custom-call | bytes 11796480 | tf_op jit(solution)/shard_map/pallas_call | solution.py:70
  160.7 18.1 %shard_map.150 = (bf16[24,256,768]{2,1,0:T(8,128)(2,1)}, f32[24,256,384]{2,1,0:T(8,128)}, f32[2,384]{1,0:T(2,128)}, f32[4,384]{1,0:T(4,128)}) custom-call(f32[24,256,384]{2,1,0:T(8,128)} %get-tuple-element.59.refs_0_.refs_2_.refs_3_.refs_1_, f32[24,256,384]{2,1,0:T(8,128)} %get-tuple-element.57.refs_4_.refs_1_, f32[2,384]{1,0:T(2,128)} %shard_map.149.refs_2_, ...), custom_call_target="tpu_custom_call" | custom-call | bytes 37748736 | tf_op jit(solution)/shard_map/pallas_call | solution.py:70
  191.5 16.8 %shard_map.151.refs_9_ = f32[1,768,384]{2,1,0:T(8,128)} custom-call(f32[24,256,768]{2,1,0:T(8,128)} %refs_0_.13, bf16[24,256,768]{2,1,0:T(8,128)(2,1)} %get-tuple-element.61.refs_1_), custom_call_target="tpu_custom_call" | custom-call | flops 10871635968 | bytes 28311552 | tf_op jit(solution)/shard_map/pallas_call | solution.py:70
  209.0 4.6 %shard_map.152 = (f32[12,64,384]{2,1,0:T(8,128)}, f32[12,64,384]{2,1,0:T(8,128)}, f32[5,384]{1,0:T(8,128)}, f32[384]{0:T(512)}, f32[384]{0:T(512)}) custom-call(f32[24,256,384]{2,1,0:T(8,128)} %get-tuple-element.62.refs_0_.refs_1_, f32[24,256,384]{2,1,0:T(8,128)} %get-tuple-element.62.refs_0_.refs_1_, ...), custom_call_target="tpu_custom_call" | custom-call | bytes 4718592 | tf_op jit(solution)/shard_map/pallas_call | solution.py:70
  213.5 3.6 collective-permute-start.36
  218.5 4.6 %shard_map.153 = (f32[12,64,384]{2,1,0:T(8,128)}, f32[12,64,384]{2,1,0:T(8,128)}) custom-call(f32[24,256,384]{2,1,0:T(8,128)} %get-tuple-element.62.refs_0_.refs_1_, f32[24,256,384]{2,1,0:T(8,128)} %get-tuple-element.62.refs_0_.refs_1_, f32[24,256,384]{2,1,0:T(8,128)} %get-tuple-element.59.refs_0_.refs_2_.refs_3_.refs_1_, ...), custom_call_target="tpu_custom_call" | custom-call | bytes 4718592 | tf_op jit(solution)/shard_map/pallas_call | solution.py:70
  224.4 5.5 %collective-permute-start.34 = (f32[12,64,384]{2,1,0:T(8,128)}, f32[12,64,384]{2,1,0:T(8,128)S(1)}, u32[]{:S(2)}, u32[]{:S(2)}) collective-permute-start(f32[12,64,384]{2,1,0:T(8,128)} %get-tuple-element.68.refs_5_), channel_id=1, source_target_pairs={{0,8},{8,16},{16,24},{1,9},{9,17},{17,25},{2,10},{10,18},{18,26},{... | collective-permute-start | bytes 3538952 | tf_op jit(solution)/shard_map/ppermute | solution.py:635
  229.8 21.8 %shard_map.154 = (f32[24,256,384]{2,1,0:T(8,128)}, f32[3,768,384]{2,1,0:T(8,128)}) custom-call(f32[24,256,384]{2,1,0:T(8,128)} %get-tuple-element.62.refs_0_.refs_1_, f32[24,256,384]{2,1,0:T(8,128)} %get-tuple-element.59.refs_0_.refs_2_.refs_3_.refs_1_, f32[5,384]{1,0:T(8,128)} %get-tuple-element.65.refs_4_.refs_2_, ...), custom_call_target="tpu_custom_call" | custom-call | flops 10871635968 | bytes 47185920 | tf_op jit(solution)/shard_map/pallas_call | solution.py:70
  252.6 17.2 %shard_map.155.refs_4_ = f32[768,768]{1,0:T(8,128)} custom-call(f32[24,256,384]{2,1,0:T(8,128)} %get-tuple-element.69.refs_0_, f32[12,64,384]{2,1,0:T(8,128)} %copy-done.4, f32[12,64,384]{2,1,0:T(8,128)} %collective-permute-done.37.refs_2_, bf16[24,256,1536]{2,1,0:T(8,128)(2,1)} %get-tuple-element.66.refs_3_, f32[3,768,384]{2,1,0:T(8,128)} %get-tuple-element.72.refs_4_.refs_5_), custom_call_target="tpu_custom_call" | custom-call | flops 10871635968 | bytes 18874368 | tf_op jit(solution)/shard_map/pallas_call | solution.py:70
  271.9 18.0 %shard_map.156.refs_3_ = f32[3,768,384]{2,1,0:T(8,128)} custom-call(f32[24,256,384]{2,1,0:T(8,128)} %get-tuple-element.69.refs_0_, f32[12,64,384]{2,1,0:T(8,128)} %copy-done.3, f32[12,64,384]{2,1,0:T(8,128)} %copy-done.2, bf16[24,256,1536]{2,1,0:T(8,128)(2,1)} %get-tuple-element.66.refs_3_, ...), custom_call_target="tpu_custom_call", output_to_operand_aliasing={{}: (5, {})} | custom-call | flops 10871635968 | bytes 18874368 | tf_op jit(solution)/shard_map/pallas_call | solution.py:70
  290.2 22.8 %shard_map.157.refs_7_ = f32[24,256,768]{2,1,0:T(8,128)} custom-call(f32[24,256,768]{2,1,0:T(8,128)} %refs_2_.3, bf16[24,256,768]{2,1,0:T(8,128)(2,1)} %get-tuple-element.61.refs_1_, f32[384,768]{1,0:T(8,128)} %refs_2_.2, f32[3,768,384]{2,1,0:T(8,128)} %shard_map.156.refs_3_), custom_call_target="tpu_custom_call" | custom-call | flops 10871635968 | bytes 47185920 | tf_op jit(solution)/shard_map/pallas_call | solution.py:70
  312.9 25.0 %shard_map.158 = (f32[24,256,768]{2,1,0:T(8,128)}, f32[2,768]{1,0:T(2,128)}) custom-call(f32[24,256,384]{2,1,0:T(8,128)} %get-tuple-element.69.refs_0_, f32[12,64,384]{2,1,0:T(8,128)} %copy-done.4, f32[12,64,384]{2,1,0:T(8,128)} %collective-permute-done.37.refs_2_, f32[24,256,768]{2,1,0:T(8,128)} %get-tuple-element.73.refs_3_, f32[24,256,768]{2,1,0:T(8,128)} %refs_2_.3, ...), custom_call_target="tpu_custom_call" | custom-call | flops 16307453952 | bytes 33030144 | tf_op jit(solution)/shard_map/pallas_call | solution.py:70
  339.9 24.8 %shard_map.159 = (f32[24,256,768]{2,1,0:T(8,128)}, f32[2,768]{1,0:T(2,128)}) custom-call(f32[24,256,384]{2,1,0:T(8,128)} %get-tuple-element.69.refs_0_, f32[12,64,384]{2,1,0:T(8,128)} %copy-done.3, f32[12,64,384]{2,1,0:T(8,128)} %copy-done.2, f32[24,256,768]{2,1,0:T(8,128)} %get-tuple-element.73.refs_3_, ...), custom_call_target="tpu_custom_call", output_to_operand_aliasing={{0}: (8, {})} | custom-call | flops 16307453952 | bytes 33030144 | tf_op jit(solution)/shard_map/pallas_call | solution.py:70
  375.7 4.0 all-reduce.2.cloned.1.call-done
  388.4 26.6 %shard_map.160 = (f32[24,256,768]{2,1,0:T(8,128)}, f32[768]{0:T(1024)}, f32[768]{0:T(1024)}) custom-call(f32[24,256,768]{2,1,0:T(8,128)} %refs_0_.13, f32[24,256,768]{2,1,0:T(8,128)} %get-tuple-element.76.refs_1_, f32[24,256,768]{2,1,0:T(8,128)} %refs_2_.3, f32[2,768]{1,0:T(2,128)} %copy-done.6, f32[2,768]{1,0:T(2,128)} %copy-done.10, f32[2,768]{1,0:T(2,128)} %copy-done.9, ...), custom_call_target="tpu_custom_call" | custom-call | bytes 75497472 | tf_op jit(solution)/shard_map/pallas_call | solution.py:70
  415.0 5.3 %all-gather.2.cloned.1.call-done = f32[4,768,384]{2,1,0:T(8,128)} async-done(((f32[4,96,384]{2,1,0:T(8,128)}), f32[4,768,384]{2,1,0:T(8,128)}) %all-gather.2.cloned.1.call-update) | async-done | bytes 4718608 | tf_op jit(solution)/shard_map/all_gather | solution.py:729
  423.0 4.0 slice.8
  (178 shorter events, 90.9 us)
Async XLA Ops:
  7.2 282.7 %reduce-scatter.3.cloned.1.call-start = ((), (), s32[]{:S(2)}) async-start(), calls=%async_computation.2 | async-start | bytes 1327104 | tf_op jit(solution)/shard_map/reduce_scatter | solution.py:615
  16.9 5.9 %collective-permute-start.6 = (f32[2,768]{1,0:T(2,128)}, f32[2,768]{1,0:T(2,128)S(1)}, u32[]{:S(2)}, u32[]{:S(2)}) collective-permute-start(f32[2,768]{1,0:T(2,128)} %shard_map.143.refs_0_), channel_id=1, source_target_pairs={{0,7},{1,0},{2,1},{3,2},{4,3},{5,4},{6,5},{7,6},{8,15},{9,8},{10,9... | collective-permute-start | bytes 18440 | tf_op jit(solution)/shard_map/ppermute | solution.py:133
  22.8 5.2 %collective-permute-start.1 = (f32[2,768]{1,0:T(2,128)}, f32[2,768]{1,0:T(2,128)S(1)}, u32[]{:S(2)}, u32[]{:S(2)}) collective-permute-start(f32[2,768]{1,0:T(2,128)} %shard_map.143.refs_0_), channel_id=1, source_target_pairs={{0,2},{1,3},{2,4},{3,5},{4,6},{5,7},{6,0},{7,1},{8,10},{9,11},{10,... | collective-permute-start | bytes 18440 | tf_op jit(solution)/shard_map/ppermute | solution.py:133
  31.4 5.2 %collective-permute-start.9 = (f32[2,768]{1,0:T(2,128)}, f32[2,768]{1,0:T(2,128)S(1)}, u32[]{:S(2)}, u32[]{:S(2)}) collective-permute-start(f32[2,768]{1,0:T(2,128)} %shard_map.144.refs_2_), channel_id=1, source_target_pairs={{0,24},{8,0},{16,8},{24,16},{1,25},{9,1},{17,9},{25,17},{2,26},{10... | collective-permute-start | bytes 18440 | tf_op jit(solution)/shard_map/ppermute | solution.py:133
  35.0 5.6 %collective-permute-start.7 = (f32[2,768]{1,0:T(2,128)}, f32[2,768]{1,0:T(2,128)S(1)}, u32[]{:S(2)}, u32[]{:S(2)}) collective-permute-start(f32[2,768]{1,0:T(2,128)} %shard_map.144.refs_2_), channel_id=1, source_target_pairs={{0,8},{8,16},{16,24},{24,0},{1,9},{9,17},{17,25},{25,1},{2,10},{10... | collective-permute-start | bytes 18440 | tf_op jit(solution)/shard_map/ppermute | solution.py:133
  69.8 37.5 %collective-permute-start.12 = (f32[12,64,384]{2,1,0:T(8,128)}, f32[12,64,384]{2,1,0:T(8,128)S(1)}, u32[]{:S(2)}, u32[]{:S(2)}) collective-permute-start(f32[12,64,384]{2,1,0:T(8,128)} %get-tuple-element.54), channel_id=1, source_target_pairs={{0,8},{8,16},{16,24},{1,9},{9,17},{17,25},{2,10},{10,18},{18,26},{... | collective-permute-start | bytes 3538952 | tf_op jit(solution)/shard_map/ppermute | solution.py:558
  71.2 36.2 %collective-permute-start.13 = (f32[12,64,384]{2,1,0:T(8,128)}, f32[12,64,384]{2,1,0:T(8,128)}, u32[]{:S(2)}, u32[]{:S(2)}) collective-permute-start(f32[12,64,384]{2,1,0:T(8,128)} %get-tuple-element.55), channel_id=1, source_target_pairs={{8,0},{16,8},{24,16},{9,1},{17,9},{25,17},{10,2},{18,10},{26,18},{... | collective-permute-start | bytes 3538952 | tf_op jit(solution)/shard_map/ppermute | solution.py:559
  101.0 27.7 %collective-permute-start.10 = (f32[12,64,384]{2,1,0:T(8,128)}, f32[12,64,384]{2,1,0:T(8,128)S(1)}, u32[]{:S(2)}, u32[]{:S(2)}) collective-permute-start(f32[12,64,384]{2,1,0:T(8,128)} %get-tuple-element.52), channel_id=1, source_target_pairs={{0,8},{8,16},{16,24},{1,9},{9,17},{17,25},{2,10},{10,18},{18,26},{... | collective-permute-start | bytes 3538952 | tf_op jit(solution)/shard_map/ppermute | solution.py:558
  105.9 26.7 %collective-permute-start.11 = (f32[12,64,384]{2,1,0:T(8,128)}, f32[12,64,384]{2,1,0:T(8,128)S(1)}, u32[]{:S(2)}, u32[]{:S(2)}) collective-permute-start(f32[12,64,384]{2,1,0:T(8,128)} %get-tuple-element.53), channel_id=1, source_target_pairs={{8,0},{16,8},{24,16},{9,1},{17,9},{25,17},{10,2},{18,10},{26,18},{... | collective-permute-start | bytes 3538952 | tf_op jit(solution)/shard_map/ppermute | solution.py:559
  140.2 5.1 %collective-permute-start.19 = (f32[2,384]{1,0:T(2,128)}, f32[2,384]{1,0:T(2,128)S(1)}, u32[]{:S(2)}, u32[]{:S(2)}) collective-permute-start(f32[2,384]{1,0:T(2,128)} %get-tuple-element.60.refs_0_), channel_id=1, source_target_pairs={{0,6},{1,7},{2,0},{3,1},{4,2},{5,3},{6,4},{7,5},{8,14},{9,15},{10,... | collective-permute-start | bytes 9224 | tf_op jit(solution)/shard_map/ppermute | solution.py:133
  154.5 5.6 %collective-permute-start.21 = (f32[2,384]{1,0:T(2,128)}, f32[2,384]{1,0:T(2,128)S(1)}, u32[]{:S(2)}, u32[]{:S(2)}) collective-permute-start(f32[2,384]{1,0:T(2,128)} %shard_map.149.refs_2_), channel_id=1, source_target_pairs={{0,8},{8,16},{16,24},{24,0},{1,9},{9,17},{17,25},{25,1},{2,10},{10... | collective-permute-start | bytes 9224 | tf_op jit(solution)/shard_map/ppermute | solution.py:133
  178.9 5.7 %collective-permute-start.29 = (f32[2,384]{1,0:T(2,128)}, f32[2,384]{1,0:T(2,128)S(1)}, u32[]{:S(2)}, u32[]{:S(2)}) collective-permute-start(f32[2,384]{1,0:T(2,128)} %get-tuple-element.63), channel_id=1, source_target_pairs={{0,6},{1,7},{2,0},{3,1},{4,2},{5,3},{6,4},{7,5},{8,14},{9,15},{10,... | collective-permute-start | bytes 9224 | tf_op jit(solution)/shard_map/ppermute | solution.py:133
  189.4 18.9 %collective-permute-start.33 = (f32[2,384]{1,0:T(2,128)S(1)}, f32[2,384]{1,0:T(2,128)S(1)}, u32[]{:S(2)}, u32[]{:S(2)}) collective-permute-start(f32[2,384]{1,0:T(2,128)S(1)} %add_add_fusion.1.refs_4_), channel_id=1, source_target_pairs={{0,24},{8,0},{16,8},{24,16},{1,25},{9,1},{17,9},{25,17},{2,26},{10... | collective-permute-start | bytes 9224 | tf_op jit(solution)/shard_map/ppermute | solution.py:133
  189.6 18.7 %collective-permute-start.32 = (f32[2,384]{1,0:T(2,128)S(1)}, f32[2,384]{1,0:T(2,128)S(1)}, u32[]{:S(2)}, u32[]{:S(2)}) collective-permute-start(f32[2,384]{1,0:T(2,128)S(1)} %add_add_fusion.1.refs_4_), channel_id=1, source_target_pairs={{0,16},{8,24},{16,0},{24,8},{1,17},{9,25},{17,1},{25,9},{2,18},{10... | collective-permute-start | bytes 9224 | tf_op jit(solution)/shard_map/ppermute | solution.py:133
  190.7 17.6 %collective-permute-start.31 = (f32[2,384]{1,0:T(2,128)S(1)}, f32[2,384]{1,0:T(2,128)S(1)}, u32[]{:S(2)}, u32[]{:S(2)}) collective-permute-start(f32[2,384]{1,0:T(2,128)S(1)} %add_add_fusion.1.refs_4_), channel_id=1, source_target_pairs={{0,8},{8,16},{16,24},{24,0},{1,9},{9,17},{17,25},{25,1},{2,10},{10... | collective-permute-start | bytes 9224 | tf_op jit(solution)/shard_map/ppermute | solution.py:133
  213.5 38.1 %collective-permute-start.36 = (f32[12,64,384]{2,1,0:T(8,128)}, f32[12,64,384]{2,1,0:T(8,128)S(1)}, u32[]{:S(2)}, u32[]{:S(2)}) collective-permute-start(f32[12,64,384]{2,1,0:T(8,128)} %get-tuple-element.70), channel_id=1, source_target_pairs={{0,8},{8,16},{16,24},{1,9},{9,17},{17,25},{2,10},{10,18},{18,26},{... | collective-permute-start | bytes 3538952 | tf_op jit(solution)/shard_map/ppermute | solution.py:635
  217.1 34.5 %collective-permute-start.37 = (f32[12,64,384]{2,1,0:T(8,128)}, f32[12,64,384]{2,1,0:T(8,128)}, u32[]{:S(2)}, u32[]{:S(2)}) collective-permute-start(f32[12,64,384]{2,1,0:T(8,128)} %get-tuple-element.71), channel_id=1, source_target_pairs={{8,0},{16,8},{24,16},{9,1},{17,9},{25,17},{10,2},{18,10},{26,18},{... | collective-permute-start | bytes 3538952 | tf_op jit(solution)/shard_map/ppermute | solution.py:636
  218.4 119.5 %reduce-scatter.5.cloned.1.call-start = ((), (), s32[]{:S(2)}) async-start(), calls=%async_computation.3 | async-start | bytes 3981312 | tf_op jit(solution)/shard_map/reduce_scatter | solution.py:681
  223.1 46.7 %collective-permute-start.35 = (f32[12,64,384]{2,1,0:T(8,128)}, f32[12,64,384]{2,1,0:T(8,128)S(1)}, u32[]{:S(2)}, u32[]{:S(2)}) collective-permute-start(f32[12,64,384]{2,1,0:T(8,128)} %get-tuple-element.67.refs_4_), channel_id=1, source_target_pairs={{8,0},{16,8},{24,16},{9,1},{17,9},{25,17},{10,2},{18,10},{26,18},{... | collective-permute-start | bytes 3538952 | tf_op jit(solution)/shard_map/ppermute | solution.py:636
  224.4 45.4 %collective-permute-start.34 = (f32[12,64,384]{2,1,0:T(8,128)}, f32[12,64,384]{2,1,0:T(8,128)S(1)}, u32[]{:S(2)}, u32[]{:S(2)}) collective-permute-start(f32[12,64,384]{2,1,0:T(8,128)} %get-tuple-element.68.refs_5_), channel_id=1, source_target_pairs={{0,8},{8,16},{16,24},{1,9},{9,17},{17,25},{2,10},{10,18},{18,26},{... | collective-permute-start | bytes 3538952 | tf_op jit(solution)/shard_map/ppermute | solution.py:635
  289.9 89.8 %all-reduce.2.cloned.1.call-start = ((), (), s32[]{:S(2)}) async-start(), calls=%async_computation.4 | async-start | bytes 1179648 | tf_op jit(solution)/shard_map/psum | solution.py:725
  339.8 80.4 %all-gather.2.cloned.1.call-start = ((), (), s32[]{:S(2)}) async-start(), calls=%async_computation.5 | async-start | bytes 5308416 | tf_op jit(solution)/shard_map/all_gather | solution.py:729
  365.0 5.8 %collective-permute-start.43 = (f32[2,768]{1,0:T(2,128)}, f32[2,768]{1,0:T(2,128)S(1)}, u32[]{:S(2)}, u32[]{:S(2)}) collective-permute-start(f32[2,768]{1,0:T(2,128)} %get-tuple-element.77), channel_id=1, source_target_pairs={{0,6},{1,7},{2,0},{3,1},{4,2},{5,3},{6,4},{7,5},{8,14},{9,15},{10,... | collective-permute-start | bytes 18440 | tf_op jit(solution)/shard_map/ppermute | solution.py:133
  382.3 5.4 %collective-permute-start.45 = (f32[2,768]{1,0:T(2,128)S(1)}, f32[2,768]{1,0:T(2,128)S(1)}, u32[]{:S(2)}, u32[]{:S(2)}) collective-permute-start(f32[2,768]{1,0:T(2,128)S(1)} %add_add_fusion.refs_3_), channel_id=1, source_target_pairs={{0,8},{8,16},{16,24},{24,0},{1,9},{9,17},{17,25},{25,1},{2,10},{10... | collective-permute-start | bytes 18440 | tf_op jit(solution)/shard_map/ppermute | solution.py:133
  (63 other events, 246.6 us)
Sparse Core Ops, SparseCore 0:
  218.6 37.7 reduce-scatter.2
  290.0 47.3 reduce-scatter.4
  340.4 39.2 all-reduce.1
  381.6 38.5 all-gather.1
